TPU v7x, 32 devices: a whole 2x2x4 slice. The times are simulated.
32 devices in a mesh: dom: 32 (over z, y, x, core).
Axes of the slice: x: 2, y: 2, z: 4, core: 2. Of those that a mesh axis runs over, the one named last changes fastest.
Arguments:
- positions: float32 [32, 3, 2048], P('dom'), may hold values from -6 to 6
- states: float32 [32, 5, 27, 256], P('dom'), may hold values from -6 to 6
- conn: int32 [32, 27, 256], P('dom'), may hold values from 0 to 2047
- send_nodes: int32 [32, 4, 32], P('dom'), may hold values from 0 to 2047
- recv_nodes: int32 [32, 4, 32], P('dom'), may hold values from 0 to 2047
- send_elems: int32 [32, 4, 16], P('dom'), may hold values from 0 to 255
- neighbours: int32 [32, 6, 256], P('dom'), may hold values from 0 to 319
- live: int32 [32], P('dom'), may hold values from 128 to 256, as said below
- smooth: float32 [27, 27], replicated, may hold values from -1.25 to 1.25
- face_geo: float32 [6, 3, 27], replicated, may hold values from -0.625 to 0.625
- rates: float32 [32, 6, 256], P('dom'), may hold values from 0.1 to 1
- stiff: float32 [27, 27], replicated, may hold values from -1.25 to 1.25
- lift: float32 [6, 27, 27], replicated, may hold values from -1.25 to 1.25
- mass_inv: float32 [27, 27], replicated, may hold values from -1.25 to 1.25
Outputs:
- coords: float32 [32, 3, 2048], P('dom')
- remapped: float32 [32, 5, 27, 256], P('dom')
Inputs may be any that keep to these rules, and one draw needn't show every extreme that they name: Elements from live[p] on are padding; at least one partition is full.
All inputs are finite; a program needn't handle non-finite values.
Results may differ from a plain program's by a relative error of at most 0.0001.
Values sent between devices are 32-bit elements; how exact they have to be, the bound alone decides.
A program may use at most 64 MiB of HBM per device.

v0:
```python
import functools

import jax
import jax.numpy as jnp
from jax import lax
from jax.experimental import pallas as pl
from jax.experimental.pallas import tpu as pltpu
from jax.sharding import PartitionSpec as P

SWEEPS = 3
STEPS = 4
CFL = 0.4
F32 = jnp.float32
BF16 = jnp.bfloat16
HIGHEST = lax.Precision.HIGHEST
MESH = pl.DeviceIdType.MESH
LANES = 128
ROWS = 32
RADIX = 32


def rounds_of(parts):
    found, stride = [], 1
    while parts > 1:
        radix = max(r for r in range(1, RADIX + 1) if parts % r == 0)
        if radix == 1:
            radix = parts
        found.append((radix, stride))
        stride *= radix
        parts //= radix
    return found


def pick(table, index):
    return jnp.take_along_axis(table, index, axis=1, mode="promise_in_bounds")


def split(x):
    high = x.astype(BF16)
    low = (x - high.astype(F32)).astype(BF16)
    return high, low


def mm(a, b):
    return jnp.dot(a, b, preferred_element_type=F32)


def mm3(a, b):
    high, low = split(b)
    return mm(a[0], high) + (mm(a[1], high) + mm(a[0], low))


def mm_nt(a, b):
    return lax.dot_general(a, b, (((1,), (1,)), ((), ())), preferred_element_type=F32)


def iota(shape, dim):
    return lax.broadcasted_iota(jnp.int32, shape, dim)


def kernel(
    parts, shifts, rounds,
    pos, states, conn, send_nodes, recv_nodes, send_elems, neighbours, live,
    smooth, face_geo, rates, stiff, lift, mass_inv,
    out_c, out_u,
    x_ref, x0_ref, s_ref, lo_ref, hi_ref, y_ref, z_ref, b_ref, rb_ref,
    u_ref, nb_ref, rate_ref, pad_ref, fg_ref, w_ref, idx_ref,
    v_send, v_recv, g_send, g_recv, m_send, m_recv,
    vs_sem, vr_sem, gs_sem, gr_sem, ms_sem, mr_sem,
):
    me = lax.axis_index("dom")
    basis, elems = conn.shape[1], conn.shape[2]
    fields = states.shape[1]
    faces = neighbours.shape[1]
    nodes = pos.shape[2]
    groups = nodes // LANES
    halves = elems // LANES
    shared = send_nodes.shape[2]
    ghosts = send_elems.shape[2]
    slots = LANES // ghosts

    partners = []
    for radix, stride in rounds:
        digit = lax.rem(me // stride, radix)
        partners.append(
            [me + (lax.rem(digit + j, radix) - digit) * stride for j in range(1, radix)]
        )
    targets = [lax.rem(me + o + parts, parts) for o in shifts]

    barrier = pltpu.get_barrier_semaphore()
    greeted = targets + [t for one in partners for t in one]
    for t in greeted:
        pl.semaphore_signal(barrier, inc=1, device_id=(t,), device_id_type=MESH)

    u_ref[...] = jnp.zeros(u_ref.shape, F32)
    for v in range(fields):
        u_ref[v * ROWS : v * ROWS + basis, :] = states[0, v]

    lane = iota((8, LANES), 1)
    row = iota((8, LANES), 0)
    idx_ref[...] = jnp.zeros(idx_ref.shape, jnp.int32)
    idx_ref[0:4, 0:shared] = send_nodes[0]
    idx_ref[8:12, 0:shared] = recv_nodes[0]
    idx_ref[16:20, 0:ghosts] = send_elems[0]

    def flat(block):
        spread = pick(block, lax.rem(lane, shared))
        kept = jnp.where(lane // shared == row, spread, 0)
        return jnp.sum(kept, axis=0, keepdims=True)

    sent_nodes = flat(idx_ref[0:8, :])
    got_nodes = flat(idx_ref[8:16, :])
    idx_ref[16:24, :] = pick(idx_ref[16:24, :], lax.rem(lane, ghosts))

    slot_of = iota((ROWS, LANES), 1) // ghosts

    def pack_ghosts(step):
        for k in range(4):
            which = jnp.broadcast_to(idx_ref[16 + k : 17 + k, :], (ROWS, LANES))
            low = which & (LANES - 1)
            far = which >> 7
            tile = jnp.zeros((ROWS, LANES), F32)
            for v in range(fields):
                got = pick(u_ref[v * ROWS : (v + 1) * ROWS, 0:LANES], low)
                for h in range(1, halves):
                    other = pick(u_ref[v * ROWS : (v + 1) * ROWS, h * LANES : (h + 1) * LANES], low)
                    got = jnp.where(far == h, other, got)
                tile = jnp.where(slot_of == (v + k) % slots, got, tile)
            g_send[step, k] = tile

    def ghost_copy(step, k):
        return pltpu.make_async_remote_copy(
            src_ref=g_send.at[step, k], dst_ref=g_recv.at[step, k],
            send_sem=gs_sem.at[step, k], recv_sem=gr_sem.at[step, k],
            device_id=(targets[k],), device_id_type=MESH,
        )

    def node_copy(sweep, k):
        return pltpu.make_async_remote_copy(
            src_ref=v_send.at[sweep], dst_ref=v_recv.at[sweep, k],
            send_sem=vs_sem.at[sweep, k], recv_sem=vr_sem.at[sweep, k],
            device_id=(targets[k],), device_id_type=MESH,
        )

    def most_copy(r, j):
        at = sum(len(p) for p in partners[:r]) + j
        return pltpu.make_async_remote_copy(
            src_ref=m_send.at[r], dst_ref=m_recv.at[at],
            send_sem=ms_sem.at[at], recv_sem=mr_sem.at[at],
            device_id=(partners[r][j],), device_id_type=MESH,
        )

    pack_ghosts(0)

    for c in range(3):
        for g in range(groups):
            r = c * groups + g
            x0_ref[r : r + 1, :] = pos[0, c : c + 1, g * LANES : (g + 1) * LANES]
    x_ref[...] = x0_ref[...]
    s_ref[...] = jnp.zeros(s_ref.shape, F32)

    alive = (iota((1, elems), 1) < live[0])
    lo_ref[...] = jnp.zeros(lo_ref.shape, jnp.int32)
    hi_ref[...] = jnp.zeros(hi_ref.shape, jnp.int32)
    lo_ref[0:basis, :] = conn[0] & (LANES - 1)
    hi_ref[0:basis, :] = conn[0] >> 7

    sub_lo = iota((LANES, elems), 0)
    sub_hi = iota((groups, elems), 0)
    one_lo, one_hi = jnp.float32(1.0), jnp.float32(1.0)
    for a in range(basis):
        at = pl.ds(a * elems, elems)
        b_ref[:, at] = jnp.where(sub_lo == lo_ref[a : a + 1, :], one_lo, 0.0).astype(BF16)
        z_ref[0:groups, at] = jnp.where(
            jnp.where(alive, hi_ref[a : a + 1, :], groups) == sub_hi, one_hi, 0.0
        ).astype(BF16)
    got_lo, got_hi = got_nodes & (LANES - 1), got_nodes >> 7
    rb_ref[...] = jnp.where(iota((LANES, LANES), 0) == got_lo, one_lo, 0.0).astype(BF16)
    got_mask = iota((groups, LANES), 0) == got_hi
    count = mm_nt(z_ref[0:groups, :], b_ref[...])
    count = count + mm_nt(jnp.where(got_mask, one_hi, 0.0).astype(BF16), rb_ref[...])
    half_inv = 0.5 / jnp.maximum(count, 1.0)
    half_inv = jnp.concatenate([half_inv] * 3, axis=0)

    pl.semaphore_wait(barrier, len(greeted))
    for k in range(4):
        ghost_copy(0, k).start()

    pad_ref[...] = jnp.zeros(pad_ref.shape, F32)
    for i in range(faces + 1):
        matrix = stiff[...] if i == 0 else lift[i - 1]
        pad_ref[i * ROWS : i * ROWS + basis, 0:basis] = jnp.dot(
            mass_inv[...], matrix, precision=HIGHEST, preferred_element_type=F32
        )
    wide = []
    for first in range(0, faces + 1, 4):
        total = None
        for i in range(first, min(first + 4, faces + 1)):
            block = pad_ref[i * ROWS : (i + 1) * ROWS, :]
            if i > first:
                block = pltpu.roll(block, ROWS * (i - first), 1)
            total = block if total is None else total + block
        wide.append(total)
    w_high, w_low = split(jnp.concatenate(wide, axis=1))
    w_ref[0:ROWS, :] = w_high
    w_ref[ROWS : 2 * ROWS, :] = w_low
    pad_ref[0:ROWS, :] = jnp.zeros((ROWS, LANES), F32)
    pad_ref[0:basis, 0:basis] = smooth[...]
    smooth_parts = split(pad_ref[0:ROWS, 0:ROWS])
    fg_ref[...] = jnp.zeros(fg_ref.shape, F32)
    for c in range(3):
        fg_ref[c * 8 : c * 8 + faces, 0:basis] = face_geo[:, c, :]

    def corners(table):
        result = []
        for c in range(3):
            cols = []
            for h in range(halves):
                low = lo_ref[:, h * LANES : (h + 1) * LANES]
                high = hi_ref[:, h * LANES : (h + 1) * LANES]
                value = jnp.zeros((ROWS, LANES), F32)
                for g in range(groups):
                    r = c * groups + g
                    source = jnp.broadcast_to(table[r : r + 1, :], (ROWS, LANES))
                    value = jnp.where(high == g, pick(source, low), value)
                cols.append(value)
            result.append(jnp.concatenate(cols, axis=1))
        return result

    s_low = jnp.broadcast_to(sent_nodes & (LANES - 1), (8, LANES))
    s_high = jnp.broadcast_to(sent_nodes >> 7, (8, LANES))

    for sweep in range(SWEEPS):
        near = corners(x_ref)
        for c in range(3):
            y = mm3(smooth_parts, near[c])
            y_high = y.astype(BF16).astype(F32)
            y_ref[c * ROWS : (c + 1) * ROWS, :] = y_high
            y_ref[(3 + c) * ROWS : (4 + c) * ROWS, :] = y - y_high
        for a in range(basis):
            at = pl.ds(a * elems, elems)
            chosen = jnp.where(alive, hi_ref[a : a + 1, :], groups) == sub_hi
            for i in range(6):
                z_ref[i * groups : (i + 1) * groups, at] = jnp.where(
                    chosen, y_ref[i * ROWS + a : i * ROWS + a + 1, :], 0.0
                ).astype(BF16)
        both = mm_nt(z_ref[...], b_ref[...])
        sums = both[0 : 3 * groups] + both[3 * groups :]
        for c in range(3):
            for g in range(groups):
                r = c * groups + g
                s_ref[g * 8 + c : g * 8 + c + 1, :] = sums[r : r + 1, :]
        picked = jnp.zeros((8, LANES), F32)
        for g in range(groups):
            picked = jnp.where(s_high == g, pick(s_ref[g * 8 : g * 8 + 8, :], s_low), picked)
        v_send[sweep] = jnp.where(row < 3, picked, 0.0)
        for k in range(4):
            node_copy(sweep, k).start()
        for k in range(4):
            node_copy(sweep, k).wait_recv()
        arrived = v_recv[sweep, 0]
        for k in range(1, 4):
            arrived = jnp.where(lane // shared == k, v_recv[sweep, k], arrived)
        arr_high = arrived.astype(BF16).astype(F32)
        arr_low = arrived - arr_high
        pieces = [
            jnp.where(got_mask, part[c : c + 1, :], 0.0).astype(BF16)
            for part in (arr_high, arr_low) for c in range(3)
        ]
        both = mm_nt(jnp.concatenate(pieces, axis=0), rb_ref[...])
        sums = sums + (both[0 : 3 * groups] + both[3 * groups :])
        x_ref[...] = 0.5 * x_ref[...] + sums * half_inv

    for c in range(3):
        for g in range(groups):
            r = c * groups + g
            out_c[0, c : c + 1, g * LANES : (g + 1) * LANES] = x_ref[r : r + 1, :]

    x_ref[...] = x_ref[...] - x0_ref[...]
    near = corners(x_ref)
    projected = jnp.zeros((8, elems), F32)
    for c in range(3):
        projected = projected + mm3(split(fg_ref[c * 8 : c * 8 + 8, 0:ROWS]), near[c])
    rate = rates[0] * (1.0 + 0.5 * jnp.tanh(projected[0:faces])) * jnp.where(alive, 1.0, 0.0)
    rate_ref[0:faces, :] = rate
    most = jnp.max(jnp.sum(rate, axis=0, keepdims=True), axis=1, keepdims=True)
    m_send[0] = jnp.broadcast_to(most, (1, LANES))
    for j in range(len(partners[0]) if rounds else 0):
        most_copy(0, j).start()

    def gather_local():
        for v in range(fields):
            for h in range(halves):
                for f in range(faces):
                    which = jnp.broadcast_to(
                        neighbours[0, f : f + 1, h * LANES : (h + 1) * LANES], (ROWS, LANES)
                    )
                    low, far = which & (LANES - 1), which >> 7
                    got = pick(u_ref[v * ROWS : (v + 1) * ROWS, 0:LANES], low)
                    for s in range(1, halves):
                        other = pick(u_ref[v * ROWS : (v + 1) * ROWS, s * LANES : (s + 1) * LANES], low)
                        got = jnp.where(far == s, other, got)
                    r = (v * faces + f) * ROWS
                    nb_ref[r : r + ROWS, h * LANES : (h + 1) * LANES] = got

    def change_of(step, v):
        ghost = g_recv[step, 0]
        for k in range(1, 4):
            ghost = jnp.where(slot_of == (v + k) % slots, g_recv[step, k], ghost)
        u = u_ref[v * ROWS : (v + 1) * ROWS, :]
        stack = [u]
        for f in range(faces):
            cols = []
            r = (v * faces + f) * ROWS
            for h in range(halves):
                which = jnp.broadcast_to(
                    neighbours[0, f : f + 1, h * LANES : (h + 1) * LANES], (ROWS, LANES)
                )
                got = pick(ghost, (which + ghosts * v) & (LANES - 1))
                cols.append(jnp.where(which >= elems, got, nb_ref[r : r + ROWS, h * LANES : (h + 1) * LANES]))
            stack.append(rate_ref[f : f + 1, :] * (jnp.concatenate(cols, axis=1) - u))
        high, low = split(jnp.concatenate(stack, axis=0))
        depth = (faces + 1) * ROWS
        first = mm(w_ref[:, 0:depth], high)
        return first[0:ROWS] + (first[ROWS:] + mm(w_ref[0:ROWS, 0:depth], low))

    for step in range(STEPS):
        if step > 0:
            pack_ghosts(step)
            for k in range(4):
                ghost_copy(step, k).start()
        gather_local()
        for k in range(4):
            ghost_copy(step, k).wait_recv()
        changes = [change_of(step, v) for v in range(fields)]
        if step == 0:
            for r, one in enumerate(partners):
                if r > 0:
                    m_send[r] = jnp.broadcast_to(most, (1, LANES))
                    for j in range(len(one)):
                        most_copy(r, j).start()
                at = sum(len(p) for p in partners[:r])
                for j in range(len(one)):
                    most_copy(r, j).wait_recv()
                tile = m_send[r]
                for j in range(len(one)):
                    tile = jnp.maximum(tile, m_recv[at + j])
                most = tile[0:1, 0:1]
            scale = jnp.where(alive, CFL / most, 0.0)
        for v in range(fields):
            new = u_ref[v * ROWS : (v + 1) * ROWS, :] + scale * changes[v]
            if step < STEPS - 1:
                u_ref[v * ROWS : (v + 1) * ROWS, :] = new
            else:
                out_u[0, v] = new[0:basis, :]

    for sweep in range(SWEEPS):
        for k in range(4):
            node_copy(sweep, k).wait_send()
    for step in range(STEPS):
        for k in range(4):
            ghost_copy(step, k).wait_send()
    for r, one in enumerate(partners):
        for j in range(len(one)):
            most_copy(r, j).wait_send()


def on_device(*args):
    pos, states, conn = args[:3]
    parts = lax.axis_size("dom")
    w = max(parts // 8, 1)
    shifts = (1, -1, w, -w)
    rounds = rounds_of(parts)
    total = sum(r - 1 for r, _ in rounds)
    basis, elems = conn.shape[1:]
    fields, faces = states.shape[1], args[6].shape[1]
    groups = pos.shape[2] // LANES
    vmem = pl.BlockSpec(memory_space=pltpu.VMEM)
    smem = pl.BlockSpec(memory_space=pltpu.SMEM)
    specs = [smem if i == 7 else vmem for i in range(len(args))]
    scratch = [
        pltpu.VMEM((3 * groups, LANES), F32),
        pltpu.VMEM((3 * groups, LANES), F32),
        pltpu.VMEM((8 * groups, LANES), F32),
        pltpu.VMEM((ROWS, elems), jnp.int32),
        pltpu.VMEM((ROWS, elems), jnp.int32),
        pltpu.VMEM((6 * ROWS, elems), F32),
        pltpu.VMEM((6 * groups, basis * elems), BF16),
        pltpu.VMEM((LANES, basis * elems), BF16),
        pltpu.VMEM((LANES, LANES), BF16),
        pltpu.VMEM((fields * ROWS, elems), F32),
        pltpu.VMEM((fields * faces * ROWS, elems), F32),
        pltpu.VMEM((8, elems), F32),
        pltpu.VMEM(((faces + 1) * ROWS, LANES), F32),
        pltpu.VMEM((24, LANES), F32),
        pltpu.VMEM((2 * ROWS, 2 * LANES), BF16),
        pltpu.VMEM((24, LANES), jnp.int32),
        pltpu.VMEM((SWEEPS, 8, LANES), F32),
        pltpu.VMEM((SWEEPS, 4, 8, LANES), F32),
        pltpu.VMEM((STEPS, 4, ROWS, LANES), F32),
        pltpu.VMEM((STEPS, 4, ROWS, LANES), F32),
        pltpu.VMEM((max(len(rounds), 1), 1, LANES), F32),
        pltpu.VMEM((max(total, 1), 1, LANES), F32),
        pltpu.SemaphoreType.DMA((SWEEPS, 4)),
        pltpu.SemaphoreType.DMA((SWEEPS, 4)),
        pltpu.SemaphoreType.DMA((STEPS, 4)),
        pltpu.SemaphoreType.DMA((STEPS, 4)),
        pltpu.SemaphoreType.DMA((max(total, 1),)),
        pltpu.SemaphoreType.DMA((max(total, 1),)),
    ]
    return pl.pallas_call(
        functools.partial(kernel, parts, shifts, rounds),
        out_shape=(
            jax.ShapeDtypeStruct(pos.shape, F32),
            jax.ShapeDtypeStruct(states.shape, F32),
        ),
        in_specs=specs,
        out_specs=(vmem, vmem),
        scratch_shapes=scratch,
        compiler_params=pltpu.CompilerParams(
            collective_id=0, has_side_effects=True, vmem_limit_bytes=32 * 1024 * 1024
        ),
    )(*args)


def solution(mesh):
    dom = lambda rank: P("dom", *([None] * (rank - 1)))
    in_specs = (
        dom(3), dom(4), dom(3), dom(3), dom(3), dom(3), dom(3), P("dom"),
        P(), P(), dom(3), P(), P(), P(),
    )
    return jax.shard_map(
        on_device, mesh=mesh, in_specs=in_specs, out_specs=(dom(3), dom(4)), check_vma=False
    )
```

profile of v0, /device:TPU:0, one launch (start us, length us, event | category | flops | bytes accessed | tf_op | source)
XLA Modules:
  0.0 54.1 jit_solution(18205697898743508265)
XLA Ops:
  0.6 0.0 copy-start.8
  1.3 0.7 %copy.19.neighbours = s32[1,6,256]{2,1,0:T(8,128)S(1)} copy(s32[1,6,256]{2,0,1:T(1,128)} %param.20) | data formatting | bytes 12288 | tf_op args[6]
  2.0 0.7 %copy.20.rates = f32[1,6,256]{2,1,0:T(8,128)S(1)} copy(f32[1,6,256]{2,0,1:T(1,128)} %param.24) | data formatting | bytes 12288 | tf_op args[10]
  2.7 0.8 %copy.16.pos = f32[1,3,2048]{2,1,0:T(4,128)S(1)} copy(f32[1,3,2048]{2,0,1:T(1,128)} %param.14) | data formatting | bytes 49152 | tf_op args[0]
  3.5 0.8 %copy.18.conn = s32[1,27,256]{2,1,0:T(8,128)S(1)} copy(s32[1,27,256]{2,0,1:T(1,128)} %param.16) | data formatting | bytes 55296 | tf_op args[2]
  4.2 0.0 copy-done.8
  4.2 0.0 copy-start
  4.2 0.0 copy-start.2
  4.2 0.0 copy-start.3
  4.3 0.0 copy-start.4
  4.3 0.0 copy-start.5
  4.3 0.0 copy-start.6
  4.3 0.0 copy-start.7
  4.3 0.8 %copy-done = f32[6,27,27]{2,1,0:T(8,128)S(1)} copy-done((f32[6,27,27]{2,1,0:T(8,128)S(1)}, f32[6,27,27]{2,1,0:T(8,128)}, u32[]{:S(2)}) %copy-start) | copy-done | bytes 17520
  5.1 0.0 copy-done.1
  5.1 0.0 copy-done.2
  5.1 0.0 copy-done.3
  5.1 0.0 copy-done.4
  5.1 0.0 copy-done.5
  5.1 0.0 copy-done.6
  5.1 0.0 copy-done.7
  5.2 47.5 %shard_map.149 = (f32[1,3,2048]{2,1,0:T(4,128)S(1)}, f32[1,5,27,256]{3,2,1,0:T(8,128)S(1)}) custom-call(f32[1,3,2048]{2,1,0:T(4,128)S(1)} %copy.16.pos, f32[1,5,27,256]{3,2,1,0:T(8,128)S(1)} %copy.17.states, s32[1,27,256]{2,1,0:T(8,128)S(1)} %copy.18.conn, s32[1,4,32]{2,1,0:T(4,128)S(1)} %copy-done.5, s32[1,4,32]{2,1,0:T(4,128)S(1)} %copy-done.6, ...), custom_call_target="tpu_custom_call" | custom-call | tf_op jit(solution)/shard_map/pallas_call | solution.py:411
  52.7 0.6 %copy.21 = f32[1,3,2048]{2,0,1:T(1,128)} copy(f32[1,3,2048]{2,1,0:T(4,128)S(1)} %get-tuple-element.2) | data formatting | bytes 49152 | tf_op jit(solution)/shard_map/pallas_call | solution.py:411
  53.3 0.8 %copy.22 = f32[1,5,27,256]{3,0,2,1:T(1,128)} copy(f32[1,5,27,256]{3,2,1,0:T(8,128)S(1)} %get-tuple-element.3) | data formatting | bytes 276480 | tf_op jit(solution)/shard_map/pallas_call | solution.py:411
  (2 shorter events, 0.0 us)
Async XLA Ops:
  0.6 3.6 %copy-start.8 = (f32[1,5,27,256]{3,0,2,1:T(1,128)S(1)}, f32[1,5,27,256]{3,0,2,1:T(1,128)}, u32[]{:S(2)}) copy-start(f32[1,5,27,256]{3,0,2,1:T(1,128)} %param.15) | copy-start | bytes 414724
  4.2 0.9 %copy-start = (f32[6,27,27]{2,1,0:T(8,128)S(1)}, f32[6,27,27]{2,1,0:T(8,128)}, u32[]{:S(2)}) copy-start(f32[6,27,27]{2,1,0:T(8,128)} %lift.1) | copy-start | bytes 52492
  4.2 0.9 %copy-start.1 = (f32[27,27]{1,0:T(8,128)S(1)}, f32[27,27]{1,0:T(8,128)}, u32[]{:S(2)}) copy-start(f32[27,27]{1,0:T(8,128)} %smooth.1) | copy-start | bytes 8752
  4.2 0.9 %copy-start.2 = (f32[27,27]{1,0:T(8,128)S(1)}, f32[27,27]{1,0:T(8,128)}, u32[]{:S(2)}) copy-start(f32[27,27]{1,0:T(8,128)} %stiff.1) | copy-start | bytes 8752
  4.2 0.9 %copy-start.3 = (f32[27,27]{1,0:T(8,128)S(1)}, f32[27,27]{1,0:T(8,128)}, u32[]{:S(2)}) copy-start(f32[27,27]{1,0:T(8,128)} %mass_inv.1) | copy-start | bytes 8752
  4.3 0.9 %copy-start.4 = (f32[6,3,27]{2,1,0:T(4,128)S(1)}, f32[6,3,27]{2,1,0:T(4,128)}, u32[]{:S(2)}) copy-start(f32[6,3,27]{2,1,0:T(4,128)} %face_geo.1) | copy-start | bytes 5836
  4.3 0.9 %copy-start.5 = (s32[1,4,32]{2,1,0:T(4,128)S(1)}, s32[1,4,32]{2,1,0:T(4,128)}, u32[]{:S(2)}) copy-start(s32[1,4,32]{2,1,0:T(4,128)} %send_nodes.1) | copy-start | bytes 1540
  4.3 0.9 %copy-start.6 = (s32[1,4,32]{2,1,0:T(4,128)S(1)}, s32[1,4,32]{2,1,0:T(4,128)}, u32[]{:S(2)}) copy-start(s32[1,4,32]{2,1,0:T(4,128)} %recv_nodes.1) | copy-start | bytes 1540
  4.3 0.9 %copy-start.7 = (s32[1,4,16]{2,1,0:T(4,128)S(1)}, s32[1,4,16]{2,1,0:T(4,128)}, u32[]{:S(2)}) copy-start(s32[1,4,16]{2,1,0:T(4,128)} %send_elems.1) | copy-start | bytes 772
where the time goes:
time: 54.5 us; the launch traced here: 54.1 us
  Pallas kernels  47.5 us (87%)
  local copies, waits for them, and re-layouts  5.17 us (9%)
  between operations  1.42 us (3%)
    pallas_call x1, Pallas kernels, on_device(): pl.pallas_call(functools.partial(kernel, parts, shifts, rounds), out_shap...  47.5 us
    unnamed x23, local copies, waits for them, and re-layouts  3.74 us
    pallas_call x2, local copies, waits for them, and re-layouts, on_device(): pl.pallas_call(functools.partial(kernel, parts, shifts, rounds), out_shap...  1.43 us

commit v1 on v0

--- a/solution.py
+++ b/solution.py
@@ -1,4 +1,5 @@
 import functools
+import math
 
 import jax
 import jax.numpy as jnp
@@ -16,7 +17,7 @@
 MESH = pl.DeviceIdType.MESH
 LANES = 128
 ROWS = 32
-RADIX = 32
+RADIX = 8
 
 
 def rounds_of(parts):
@@ -60,24 +61,37 @@
 
 def kernel(
     parts, shifts, rounds,
-    pos, states, conn, send_nodes, recv_nodes, send_elems, neighbours, live,
-    smooth, face_geo, rates, stiff, lift, mass_inv,
+    basis, elems, fields, faces, nodes,
+    pos_any, states_any, conn_any, send_nodes_any, recv_nodes_any, send_elems_any, neighbours_any, live,
+    smooth_any, face_geo_any, rates_any, stiff_any, lift_any, mass_inv_any,
     out_c, out_u,
-    x_ref, x0_ref, s_ref, lo_ref, hi_ref, y_ref, z_ref, b_ref, rb_ref,
+    x0_ref, states, conn, send_nodes, recv_nodes, send_elems, neighbours,
+    smooth, face_geo, rates, stiff, lift, mass_inv, in_sem,
+    x_ref, s_ref, lo_ref, hi_ref, y_ref, z_ref, b_ref, rb_ref,
     u_ref, nb_ref, rate_ref, pad_ref, fg_ref, w_ref, idx_ref,
     v_send, v_recv, g_send, g_recv, m_send, m_recv,
     vs_sem, vr_sem, gs_sem, gr_sem, ms_sem, mr_sem,
 ):
     me = lax.axis_index("dom")
-    basis, elems = conn.shape[1], conn.shape[2]
-    fields = states.shape[1]
-    faces = neighbours.shape[1]
-    nodes = pos.shape[2]
     groups = nodes // LANES
     halves = elems // LANES
-    shared = send_nodes.shape[2]
-    ghosts = send_elems.shape[2]
+    shared = send_nodes.shape[1]
+    ghosts = send_elems.shape[1]
     slots = LANES // ghosts
+
+    sources = (
+        conn_any, pos_any, states_any, send_elems_any, send_nodes_any, recv_nodes_any, smooth_any,
+        neighbours_any, rates_any, face_geo_any, mass_inv_any, stiff_any, lift_any,
+    )
+    places = (
+        conn, x0_ref, states, send_elems, send_nodes, recv_nodes, smooth,
+        neighbours, rates, face_geo, mass_inv, stiff, lift,
+    )
+    loads = [
+        pltpu.make_async_copy(a, b, in_sem.at[i]) for i, (a, b) in enumerate(zip(sources, places))
+    ]
+    for one in loads:
+        one.start()
 
     partners = []
     for radix, stride in rounds:
@@ -92,16 +106,19 @@
     for t in greeted:
         pl.semaphore_signal(barrier, inc=1, device_id=(t,), device_id_type=MESH)
 
-    u_ref[...] = jnp.zeros(u_ref.shape, F32)
+    u_ref[0] = jnp.zeros(u_ref.shape[1:], F32)
+    for one in loads:
+        one.wait()
     for v in range(fields):
-        u_ref[v * ROWS : v * ROWS + basis, :] = states[0, v]
+        for h in range(halves):
+            u_ref[0, v * ROWS : v * ROWS + basis, h * LANES : (h + 1) * LANES] = states[v * basis : (v + 1) * basis, h, :]
 
     lane = iota((8, LANES), 1)
     row = iota((8, LANES), 0)
     idx_ref[...] = jnp.zeros(idx_ref.shape, jnp.int32)
-    idx_ref[0:4, 0:shared] = send_nodes[0]
-    idx_ref[8:12, 0:shared] = recv_nodes[0]
-    idx_ref[16:20, 0:ghosts] = send_elems[0]
+    idx_ref[0:4, 0:shared] = send_nodes[...]
+    idx_ref[8:12, 0:shared] = recv_nodes[...]
+    idx_ref[16:20, 0:ghosts] = send_elems[...]
 
     def flat(block):
         spread = pick(block, lax.rem(lane, shared))
@@ -121,9 +138,9 @@
             far = which >> 7
             tile = jnp.zeros((ROWS, LANES), F32)
             for v in range(fields):
-                got = pick(u_ref[v * ROWS : (v + 1) * ROWS, 0:LANES], low)
+                got = pick(u_ref[step, v * ROWS : (v + 1) * ROWS, 0:LANES], low)
                 for h in range(1, halves):
-                    other = pick(u_ref[v * ROWS : (v + 1) * ROWS, h * LANES : (h + 1) * LANES], low)
+                    other = pick(u_ref[step, v * ROWS : (v + 1) * ROWS, h * LANES : (h + 1) * LANES], low)
                     got = jnp.where(far == h, other, got)
                 tile = jnp.where(slot_of == (v + k) % slots, got, tile)
             g_send[step, k] = tile
@@ -152,18 +169,16 @@
 
     pack_ghosts(0)
 
-    for c in range(3):
-        for g in range(groups):
-            r = c * groups + g
-            x0_ref[r : r + 1, :] = pos[0, c : c + 1, g * LANES : (g + 1) * LANES]
     x_ref[...] = x0_ref[...]
     s_ref[...] = jnp.zeros(s_ref.shape, F32)
 
     alive = (iota((1, elems), 1) < live[0])
     lo_ref[...] = jnp.zeros(lo_ref.shape, jnp.int32)
     hi_ref[...] = jnp.zeros(hi_ref.shape, jnp.int32)
-    lo_ref[0:basis, :] = conn[0] & (LANES - 1)
-    hi_ref[0:basis, :] = conn[0] >> 7
+    for h in range(halves):
+        part = conn[:, h, :]
+        lo_ref[0:basis, h * LANES : (h + 1) * LANES] = part & (LANES - 1)
+        hi_ref[0:basis, h * LANES : (h + 1) * LANES] = part >> 7
 
     sub_lo = iota((LANES, elems), 0)
     sub_hi = iota((groups, elems), 0)
@@ -271,34 +286,32 @@
         sums = sums + (both[0 : 3 * groups] + both[3 * groups :])
         x_ref[...] = 0.5 * x_ref[...] + sums * half_inv
 
-    for c in range(3):
-        for g in range(groups):
-            r = c * groups + g
-            out_c[0, c : c + 1, g * LANES : (g + 1) * LANES] = x_ref[r : r + 1, :]
+    out_c[...] = x_ref[...]
 
     x_ref[...] = x_ref[...] - x0_ref[...]
     near = corners(x_ref)
     projected = jnp.zeros((8, elems), F32)
     for c in range(3):
         projected = projected + mm3(split(fg_ref[c * 8 : c * 8 + 8, 0:ROWS]), near[c])
-    rate = rates[0] * (1.0 + 0.5 * jnp.tanh(projected[0:faces])) * jnp.where(alive, 1.0, 0.0)
+    base = jnp.concatenate([rates[:, h, :] for h in range(halves)], axis=1)
+    rate = base * (1.0 + 0.5 * jnp.tanh(projected[0:faces])) * jnp.where(alive, 1.0, 0.0)
     rate_ref[0:faces, :] = rate
     most = jnp.max(jnp.sum(rate, axis=0, keepdims=True), axis=1, keepdims=True)
     m_send[0] = jnp.broadcast_to(most, (1, LANES))
     for j in range(len(partners[0]) if rounds else 0):
         most_copy(0, j).start()
 
-    def gather_local():
+    def gather_local(step):
         for v in range(fields):
             for h in range(halves):
                 for f in range(faces):
                     which = jnp.broadcast_to(
-                        neighbours[0, f : f + 1, h * LANES : (h + 1) * LANES], (ROWS, LANES)
+                        neighbours[f, h : h + 1, :], (ROWS, LANES)
                     )
                     low, far = which & (LANES - 1), which >> 7
-                    got = pick(u_ref[v * ROWS : (v + 1) * ROWS, 0:LANES], low)
+                    got = pick(u_ref[step, v * ROWS : (v + 1) * ROWS, 0:LANES], low)
                     for s in range(1, halves):
-                        other = pick(u_ref[v * ROWS : (v + 1) * ROWS, s * LANES : (s + 1) * LANES], low)
+                        other = pick(u_ref[step, v * ROWS : (v + 1) * ROWS, s * LANES : (s + 1) * LANES], low)
                         got = jnp.where(far == s, other, got)
                     r = (v * faces + f) * ROWS
                     nb_ref[r : r + ROWS, h * LANES : (h + 1) * LANES] = got
@@ -307,14 +320,14 @@
         ghost = g_recv[step, 0]
         for k in range(1, 4):
             ghost = jnp.where(slot_of == (v + k) % slots, g_recv[step, k], ghost)
-        u = u_ref[v * ROWS : (v + 1) * ROWS, :]
+        u = u_ref[step, v * ROWS : (v + 1) * ROWS, :]
         stack = [u]
         for f in range(faces):
             cols = []
             r = (v * faces + f) * ROWS
             for h in range(halves):
                 which = jnp.broadcast_to(
-                    neighbours[0, f : f + 1, h * LANES : (h + 1) * LANES], (ROWS, LANES)
+                    neighbours[f, h : h + 1, :], (ROWS, LANES)
                 )
                 got = pick(ghost, (which + ghosts * v) & (LANES - 1))
                 cols.append(jnp.where(which >= elems, got, nb_ref[r : r + ROWS, h * LANES : (h + 1) * LANES]))
@@ -324,35 +337,44 @@
         first = mm(w_ref[:, 0:depth], high)
         return first[0:ROWS] + (first[ROWS:] + mm(w_ref[0:ROWS, 0:depth], low))
 
+    def finish_round(r, most):
+        at = sum(len(p) for p in partners[:r])
+        tile = m_send[r]
+        for j in range(len(partners[r])):
+            most_copy(r, j).wait_recv()
+            tile = jnp.maximum(tile, m_recv[at + j])
+        most = tile[0:1, 0:1]
+        if r + 1 < len(partners):
+            m_send[r + 1] = jnp.broadcast_to(most, (1, LANES))
+            for j in range(len(partners[r + 1])):
+                most_copy(r + 1, j).start()
+        return most
+
+    keep = jnp.where(alive, 1.0, 0.0)
     for step in range(STEPS):
         if step > 0:
             pack_ghosts(step)
             for k in range(4):
                 ghost_copy(step, k).start()
-        gather_local()
+        gather_local(step)
         for k in range(4):
             ghost_copy(step, k).wait_recv()
-        changes = [change_of(step, v) for v in range(fields)]
-        if step == 0:
-            for r, one in enumerate(partners):
-                if r > 0:
-                    m_send[r] = jnp.broadcast_to(most, (1, LANES))
-                    for j in range(len(one)):
-                        most_copy(r, j).start()
-                at = sum(len(p) for p in partners[:r])
-                for j in range(len(one)):
-                    most_copy(r, j).wait_recv()
-                tile = m_send[r]
-                for j in range(len(one)):
-                    tile = jnp.maximum(tile, m_recv[at + j])
-                most = tile[0:1, 0:1]
-            scale = jnp.where(alive, CFL / most, 0.0)
+        if 0 < step <= len(partners):
+            most = finish_round(step - 1, most)
         for v in range(fields):
-            new = u_ref[v * ROWS : (v + 1) * ROWS, :] + scale * changes[v]
-            if step < STEPS - 1:
-                u_ref[v * ROWS : (v + 1) * ROWS, :] = new
-            else:
-                out_u[0, v] = new[0:basis, :]
+            u_ref[step + 1, v * ROWS : (v + 1) * ROWS, :] = keep * change_of(step, v)
+    for r in range(STEPS - 1, len(partners)):
+        most = finish_round(r, most)
+    scale = jnp.broadcast_to(CFL / most, (ROWS, elems))
+    for v in range(fields):
+        term = [u_ref[k, v * ROWS : (v + 1) * ROWS, :] for k in range(STEPS + 1)]
+        new = term[STEPS]
+        for k in range(STEPS - 1, -1, -1):
+            new = math.comb(STEPS, k) * term[k] + scale * new
+        for h in range(halves):
+            out_u[v * basis : (v + 1) * basis, h, :] = new[
+                0:basis, h * LANES : (h + 1) * LANES
+            ]
 
     for sweep in range(SWEEPS):
         for k in range(4):
@@ -363,6 +385,22 @@
     for r, one in enumerate(partners):
         for j in range(len(one)):
             most_copy(r, j).wait_send()
+
+
+def hand_over(coords, remapped, out_c, out_u, held_c, held_u, sem):
+    half = remapped.shape[0] // 2
+    parts = [(coords, held_c, out_c)]
+    for at in (pl.ds(0, half), pl.ds(half, remapped.shape[0] - half)):
+        parts.append((remapped.at[at], held_u.at[at], out_u.at[at]))
+    reads = [pltpu.make_async_copy(a, b, sem.at[0, i]) for i, (a, b, _) in enumerate(parts)]
+    writes = [pltpu.make_async_copy(b, c, sem.at[1, i]) for i, (_, b, c) in enumerate(parts)]
+    for one in reads:
+        one.start()
+    for read, write in zip(reads, writes):
+        read.wait()
+        write.start()
+    for one in writes:
+        one.wait()
 
 
 def on_device(*args):
@@ -375,11 +413,20 @@
     basis, elems = conn.shape[1:]
     fields, faces = states.shape[1], args[6].shape[1]
     groups = pos.shape[2] // LANES
+    nodes = pos.shape[2]
+    halves = elems // LANES
+    flat = list(args)
+    for i, rows in ((0, 3 * groups), (1, fields * basis * halves), (2, basis * halves), (6, faces * halves), (10, faces * halves)):
+        flat[i] = args[i].reshape(rows, LANES) if i == 0 else args[i].reshape(rows // halves, halves, LANES)
+    for i in (3, 4, 5):
+        flat[i] = args[i][0]
     vmem = pl.BlockSpec(memory_space=pltpu.VMEM)
     smem = pl.BlockSpec(memory_space=pltpu.SMEM)
-    specs = [smem if i == 7 else vmem for i in range(len(args))]
-    scratch = [
-        pltpu.VMEM((3 * groups, LANES), F32),
+    hbm = pl.BlockSpec(memory_space=pl.ANY)
+    specs = [smem if i == 7 else hbm for i in range(len(args))]
+    held = [pltpu.VMEM(a.shape, a.dtype) for i, a in enumerate(flat) if i != 7]
+    scratch = held + [
+        pltpu.SemaphoreType.DMA((len(held),)),
         pltpu.VMEM((3 * groups, LANES), F32),
         pltpu.VMEM((8 * groups, LANES), F32),
         pltpu.VMEM((ROWS, elems), jnp.int32),
@@ -388,7 +435,7 @@
         pltpu.VMEM((6 * groups, basis * elems), BF16),
         pltpu.VMEM((LANES, basis * elems), BF16),
         pltpu.VMEM((LANES, LANES), BF16),
-        pltpu.VMEM((fields * ROWS, elems), F32),
+        pltpu.VMEM((STEPS + 1, fields * ROWS, elems), F32),
         pltpu.VMEM((fields * faces * ROWS, elems), F32),
         pltpu.VMEM((8, elems), F32),
         pltpu.VMEM(((faces + 1) * ROWS, LANES), F32),
@@ -408,19 +455,35 @@
         pltpu.SemaphoreType.DMA((max(total, 1),)),
         pltpu.SemaphoreType.DMA((max(total, 1),)),
     ]
-    return pl.pallas_call(
-        functools.partial(kernel, parts, shifts, rounds),
+    coords, remapped = pl.pallas_call(
+        functools.partial(kernel, parts, shifts, rounds, basis, elems, fields, faces, nodes),
         out_shape=(
-            jax.ShapeDtypeStruct(pos.shape, F32),
-            jax.ShapeDtypeStruct(states.shape, F32),
+            jax.ShapeDtypeStruct((3 * groups, LANES), F32),
+            jax.ShapeDtypeStruct((fields * basis, halves, LANES), F32),
         ),
         in_specs=specs,
         out_specs=(vmem, vmem),
         scratch_shapes=scratch,
         compiler_params=pltpu.CompilerParams(
-            collective_id=0, has_side_effects=True, vmem_limit_bytes=32 * 1024 * 1024
+            collective_id=0, has_side_effects=True, vmem_limit_bytes=60 * 1024 * 1024
         ),
-    )(*args)
+    )(*flat)
+    coords, remapped = pl.pallas_call(
+        hand_over,
+        out_shape=(
+            jax.ShapeDtypeStruct(coords.shape, F32),
+            jax.ShapeDtypeStruct(remapped.shape, F32),
+        ),
+        in_specs=[hbm, hbm],
+        out_specs=(hbm, hbm),
+        scratch_shapes=[
+            pltpu.VMEM(coords.shape, F32),
+            pltpu.VMEM(remapped.shape, F32),
+            pltpu.SemaphoreType.DMA((2, 3)),
+        ],
+        compiler_params=pltpu.CompilerParams(vmem_limit_bytes=60 * 1024 * 1024),
+    )(coords, remapped)
+    return coords.reshape(pos.shape), remapped.reshape(states.shape)
 
 
 def solution(mesh):

time: 54.5 us -> 49 us (0.90)
  local copies, waits for them, and re-layouts: 5.17 us -> 0 us
    unnamed x23 -> x0, local copies, waits for them, and re-layouts: 3.74 us -> none
    pallas_call x2 -> x0, local copies, waits for them, and re-layouts: 1.43 us -> none  [on_device(): pl.pallas_call(functools.partial(kernel, parts, shifts, rounds), out_shap...]
    pallas_call x1 -> x2, Pallas kernels: 47.5 us -> 47.5 us  [the longest x1 45.9 us: on_device(): pl.pallas_call(functools.partial(kernel, parts, shifts, rounds, basis, el...]
where the time goes in v1:
time: 49 us; the launch traced here: 48.8 us
  Pallas kernels  47.5 us (97%)
  between operations  1.29 us (3%)
    pallas_call x1, Pallas kernels, on_device(): pl.pallas_call(functools.partial(kernel, parts, shifts, rounds, basis, el...  45.9 us
    pallas_call x1, Pallas kernels, on_device(): pl.pallas_call(hand_over, out_shape=(jax.ShapeDtypeStruct(coords.shape, F...  1.62 us

profile of v1, /device:TPU:0, one launch (start us, length us, event | category | flops | bytes accessed | tf_op | source)
XLA Modules:
  0.0 48.8 jit_solution(16389927871101153737)
XLA Ops:
  1.3 45.9 %shard_map.149 = (f32[48,128]{1,0:T(8,128)}, f32[135,2,128]{2,1,0:T(2,128)}) custom-call(f32[48,128]{1,0:T(8,128)} %bitcast.12, f32[135,2,128]{2,1,0:T(2,128)} %bitcast.10, s32[27,2,128]{2,1,0:T(2,128)} %bitcast.11, s32[4,32]{1,0:T(4,128)} %bitcast.15, s32[4,32]{1,0:T(4,128)} %bitcast.16, s32[4,16]{1,0:T(4,128)} %bitcast.17, s32[6,2,128]{2,1,0:T(2,128)} %bitcast.13, ...), custom_call_target="tpu_custom_call" | custom-call | tf_op jit(solution)/shard_map/pallas_call | solution.py:458
  47.2 1.6 %shard_map.150 = (f32[48,128]{1,0:T(8,128)}, f32[135,2,128]{2,1,0:T(2,128)}) custom-call(f32[48,128]{1,0:T(8,128)} %get-tuple-element.6.coords, f32[135,2,128]{2,1,0:T(2,128)} %get-tuple-element.7.remapped), custom_call_target="tpu_custom_call" | custom-call | tf_op jit(solution)/shard_map/pallas_call | solution.py:471

commit v2 on v1

v2 whole, which is shorter than its diff:
```python
import functools
import math

import jax
import jax.numpy as jnp
from jax import lax
from jax.experimental import pallas as pl
from jax.experimental.pallas import tpu as pltpu
from jax.sharding import PartitionSpec as P

SWEEPS = 3
STEPS = 4
CFL = 0.4
F32 = jnp.float32
BF16 = jnp.bfloat16
HIGHEST = lax.Precision.HIGHEST
MESH = pl.DeviceIdType.MESH
LANES = 128
ROWS = 32
RADIX = 8


def rounds_of(parts):
    found, stride = [], 1
    while parts > 1:
        radix = max(r for r in range(1, RADIX + 1) if parts % r == 0)
        if radix == 1:
            radix = parts
        found.append((radix, stride))
        stride *= radix
        parts //= radix
    return found


def pick(table, index):
    return jnp.take_along_axis(table, index, axis=1, mode="promise_in_bounds")


def split(x):
    high = x.astype(BF16)
    low = (x - high.astype(F32)).astype(BF16)
    return high, low


def mm(a, b):
    return jnp.dot(a, b, preferred_element_type=F32)


def mm3(a, b):
    high, low = split(b)
    return mm(a[0], high) + (mm(a[1], high) + mm(a[0], low))


def mm_nt(a, b):
    return lax.dot_general(a, b, (((1,), (1,)), ((), ())), preferred_element_type=F32)


def iota(shape, dim):
    return lax.broadcasted_iota(jnp.int32, shape, dim)


def kernel(
    parts, shifts, rounds,
    basis, elems, fields, faces, nodes,
    pos_any, states_any, conn_any, send_nodes_any, recv_nodes_any, send_elems_any, neighbours_any, live,
    smooth_any, face_geo_any, rates_any, stiff_any, lift_any, mass_inv_any,
    out_c, out_u,
    x0_ref, states, conn, send_nodes, recv_nodes, send_elems, neighbours,
    smooth, face_geo, rates, stiff, lift, mass_inv, in_sem,
    x_ref, s_ref, lo_ref, hi_ref, y_ref, z_ref, b_ref, rb_ref,
    u_ref, nb_ref, rate_ref, pad_ref, fg_ref, w_ref, idx_ref,
    mv_ref, yr_ref, yw_ref, gs_ref, sl_ref, st_ref, gt_ref, nl_ref, nbs_ref, rs_ref, nbp_ref,
    v_send, v_recv, g_send, g_recv, m_send, m_recv,
    vs_sem, vr_sem, gs_sem, gr_sem, ms_sem, mr_sem,
):
    me = lax.axis_index("dom")
    groups = nodes // LANES
    halves = elems // LANES
    shared = send_nodes.shape[1]
    ghosts = send_elems.shape[1]
    slots = LANES // ghosts

    sources = (
        conn_any, pos_any, states_any, send_elems_any, send_nodes_any, recv_nodes_any, smooth_any,
        neighbours_any, rates_any, face_geo_any, mass_inv_any, stiff_any, lift_any,
    )
    places = (
        conn, x0_ref, states, send_elems, send_nodes, recv_nodes, smooth,
        neighbours, rates, face_geo, mass_inv, stiff, lift,
    )
    loads = [
        pltpu.make_async_copy(a, b, in_sem.at[i]) for i, (a, b) in enumerate(zip(sources, places))
    ]
    for one in loads:
        one.start()

    partners = []
    for radix, stride in rounds:
        digit = lax.rem(me // stride, radix)
        partners.append(
            [me + (lax.rem(digit + j, radix) - digit) * stride for j in range(1, radix)]
        )
    targets = [lax.rem(me + o + parts, parts) for o in shifts]

    barrier = pltpu.get_barrier_semaphore()
    greeted = targets + [t for one in partners for t in one]
    for t in greeted:
        pl.semaphore_signal(barrier, inc=1, device_id=(t,), device_id_type=MESH)

    def node_copy(sweep, k):
        return pltpu.make_async_remote_copy(
            src_ref=v_send.at[sweep], dst_ref=v_recv.at[sweep, k],
            send_sem=vs_sem.at[sweep, k], recv_sem=vr_sem.at[sweep, k],
            device_id=(targets[k],), device_id_type=MESH,
        )

    def ghost_copy(step, k):
        return pltpu.make_async_remote_copy(
            src_ref=g_send.at[step, k], dst_ref=g_recv.at[step, k],
            send_sem=gs_sem.at[step, k], recv_sem=gr_sem.at[step, k],
            device_id=(targets[k],), device_id_type=MESH,
        )

    def most_copy(r, j):
        at = sum(len(p) for p in partners[:r]) + j
        return pltpu.make_async_remote_copy(
            src_ref=m_send.at[r], dst_ref=m_recv.at[at],
            send_sem=ms_sem.at[at], recv_sem=mr_sem.at[at],
            device_id=(partners[r][j],), device_id_type=MESH,
        )

    lane = iota((8, LANES), 1)
    row = iota((8, LANES), 0)
    slot_of = iota((ROWS, LANES), 1) // ghosts
    tiles = (fields + 1) // 2

    idx_ref[...] = jnp.zeros(idx_ref.shape, jnp.int32)
    lo_ref[...] = jnp.zeros(lo_ref.shape, jnp.int32)
    hi_ref[...] = jnp.zeros(hi_ref.shape, jnp.int32)
    s_ref[...] = jnp.zeros(s_ref.shape, F32)
    u_ref[0] = jnp.zeros(u_ref.shape[1:], F32)
    yr_ref[...] = jnp.zeros(yr_ref.shape, F32)
    pad_ref[...] = jnp.zeros(pad_ref.shape, F32)
    fg_ref[...] = jnp.zeros(fg_ref.shape, F32)
    nbp_ref[...] = jnp.zeros(nbp_ref.shape, jnp.int32)
    rate_ref[...] = jnp.zeros(rate_ref.shape, F32)
    alive = iota((1, elems), 1) < live[0]
    for one in loads:
        one.wait()

    pad_ref[0:basis, 0:basis] = smooth[...]
    smooth_parts = split(pad_ref[0:ROWS, 0:ROWS])
    idx_ref[0:4, 0:shared] = send_nodes[...]
    idx_ref[8:12, 0:shared] = recv_nodes[...]
    idx_ref[16:20, 0:ghosts] = send_elems[...]

    def flat(block, width, count):
        spread = pick(block, lax.rem(lane, width))
        kept = jnp.where(lax.rem(lane // width, count) == row, spread, 0)
        return jnp.sum(kept, axis=0, keepdims=True)

    sent_nodes = flat(idx_ref[0:8, :], shared, 4)
    got_nodes = flat(idx_ref[8:16, :], shared, 4)

    for h in range(halves):
        part = conn[:, h, :]
        lo_ref[0:basis, h * LANES : (h + 1) * LANES] = part & (LANES - 1)
        hi_ref[0:basis, h * LANES : (h + 1) * LANES] = part >> 7

    sub_lo = iota((LANES, elems), 0)
    sub_hi = iota((groups, elems), 0)
    one_lo, one_hi = jnp.float32(1.0), jnp.float32(1.0)
    for a in range(basis):
        at = pl.ds(a * elems, elems)
        b_ref[:, at] = jnp.where(sub_lo == lo_ref[a : a + 1, :], one_lo, 0.0).astype(BF16)

    def corners(row_of, count):
        result = []
        for c in range(count):
            cols = []
            for h in range(halves):
                low = lo_ref[:, h * LANES : (h + 1) * LANES]
                high = hi_ref[:, h * LANES : (h + 1) * LANES]
                value = None
                for g in range(groups):
                    source = jnp.broadcast_to(row_of(c * groups + g), (ROWS, LANES))
                    got = pick(source, low)
                    value = got if value is None else jnp.where(high == g, got, value)
                cols.append(value)
            result.append(jnp.concatenate(cols, axis=1))
        return result

    def scatter(ys):
        for c in range(3):
            y_high = ys[c].astype(BF16).astype(F32)
            y_ref[c * ROWS : (c + 1) * ROWS, :] = y_high
            y_ref[(3 + c) * ROWS : (4 + c) * ROWS, :] = ys[c] - y_high
        for a in range(basis):
            at = pl.ds(a * elems, elems)
            chosen = jnp.where(alive, hi_ref[a : a + 1, :], groups) == sub_hi
            for i in range(6):
                z_ref[i * groups : (i + 1) * groups, at] = jnp.where(
                    chosen, y_ref[i * ROWS + a : i * ROWS + a + 1, :], 0.0
                ).astype(BF16)
        both = mm_nt(z_ref[...], b_ref[...])
        return both[0 : 3 * groups] + both[3 * groups :]

    s_low = jnp.broadcast_to(sent_nodes & (LANES - 1), (8, LANES))
    s_high = jnp.broadcast_to(sent_nodes >> 7, (8, LANES))

    def at_sent(sums):
        for c in range(3):
            for g in range(groups):
                r = c * groups + g
                s_ref[g * 8 + c : g * 8 + c + 1, :] = sums[r : r + 1, :]
        picked = jnp.zeros((8, LANES), F32)
        for g in range(groups):
            picked = jnp.where(s_high == g, pick(s_ref[g * 8 : g * 8 + 8, :], s_low), picked)
        return jnp.where(row < 3, picked, 0.0)

    def smoothed(near):
        return [mm3(smooth_parts, near[c]) for c in range(3)]

    def send_sums(sweep, value):
        v_send[sweep] = value
        for k in range(4):
            node_copy(sweep, k).start()

    sums = scatter(smoothed(corners(lambda r: x0_ref[r : r + 1, :], 3)))
    first_sent = at_sent(sums)
    pl.semaphore_wait(barrier, len(greeted))
    send_sums(0, first_sent)

    for v in range(fields):
        for h in range(halves):
            u_ref[0, v * ROWS : v * ROWS + basis, h * LANES : (h + 1) * LANES] = states[
                v * basis : (v + 1) * basis, h, :
            ]
    sent_elems = jnp.broadcast_to(flat(idx_ref[16:24, :], ghosts, 4), (8, LANES))
    sent_tile = [sent_elems]
    for t in range(1, tiles):
        sent_tile.append(pltpu.roll(sent_elems, ghosts * t, 1))
    first_of = [((slot_of + (slots - t)) & (slots - 1)) < 4 for t in range(tiles)]

    def choose(level, t, low, far):
        result = None
        for v in range(2 * t, min(2 * t + 2, fields)):
            got = None
            for h in range(halves):
                one = pick(u_ref[level, v * ROWS : (v + 1) * ROWS, h * LANES : (h + 1) * LANES], low)
                got = one if got is None else jnp.where(far == h, one, got)
            result = got if result is None else jnp.where(first_of[t], result, got)
        return result

    def send_ghosts(step):
        for k in range(4):
            tile = st_ref[step, 0]
            for t in range(1, tiles):
                tile = jnp.where(((slot_of + (slots - k)) & 3) == t, st_ref[step, t], tile)
            g_send[step, k] = tile
        for k in range(4):
            ghost_copy(step, k).start()

    for t in range(tiles):
        which = jnp.broadcast_to(sent_tile[t][0:1, :], (ROWS, LANES))
        st_ref[0, t] = choose(0, t, which & (LANES - 1), which >> 7)
    send_ghosts(0)

    got_lo, got_hi = got_nodes & (LANES - 1), got_nodes >> 7
    rb_ref[...] = jnp.where(iota((LANES, LANES), 0) == got_lo, one_lo, 0.0).astype(BF16)
    got_mask = iota((groups, LANES), 0) == got_hi
    for a in range(basis):
        at = pl.ds(a * elems, elems)
        z_ref[0:groups, at] = jnp.where(
            jnp.where(alive, hi_ref[a : a + 1, :], groups) == sub_hi, one_hi, 0.0
        ).astype(BF16)
    count = mm_nt(z_ref[0:groups, :], b_ref[...])
    count = count + mm_nt(jnp.where(got_mask, one_hi, 0.0).astype(BF16), rb_ref[...])
    half_inv = 0.5 / jnp.maximum(count, 1.0)
    hi_at_got = jnp.zeros((8, LANES), F32)
    got_lo8 = jnp.broadcast_to(got_lo, (8, LANES))
    got_hi8 = jnp.broadcast_to(got_hi, (8, LANES))
    for g in range(groups):
        hi_at_got = jnp.where(
            got_hi8 == g, pick(jnp.broadcast_to(half_inv[g : g + 1, :], (8, LANES)), got_lo8), hi_at_got
        )
    half_inv = jnp.concatenate([half_inv] * 3, axis=0)

    x_ref[...] = 0.5 * x0_ref[...] + sums * half_inv
    ahead = scatter(smoothed(corners(lambda r: x_ref[r : r + 1, :], 3)))
    ahead_sent = at_sent(ahead)

    square = (LANES, LANES)
    got_row = jnp.broadcast_to(got_nodes, square)
    got_col = jnp.transpose(got_row)
    sent_col = jnp.transpose(jnp.broadcast_to(sent_nodes, square))
    same = jnp.where(got_row == got_col, one_lo, 0.0).astype(BF16)
    marked = jnp.where((got_col & (LANES - 1)) == iota(square, 1), iota(square, 0) + 1, 0)
    col_hi = got_col >> 7
    table = [
        jnp.max(jnp.where(col_hi == g, marked, 0), axis=0, keepdims=True) for g in range(groups)
    ]
    sl_ref[...] = corners(lambda r: table[r], 1)[0]
    sent_wide = jnp.concatenate([sent_col] * halves, axis=1)
    for a in range(basis):
        node = jnp.where(alive, (hi_ref[a : a + 1, :] << 7) + lo_ref[a : a + 1, :], -1)
        gs_ref[:, pl.ds(a * elems, elems)] = jnp.where(sent_wide == node, one_lo, 0.0).astype(BF16)

    def gathered(sweep):
        for k in range(4):
            node_copy(sweep, k).wait_recv()
        arrived = v_recv[sweep, 0]
        for k in range(1, 4):
            arrived = jnp.where(lane // shared == k, v_recv[sweep, k], arrived)
        high, low = split(arrived)
        spread = (mm(high, same) + mm(low, same)) * hi_at_got
        near = []
        for c in range(3):
            cols = []
            for h in range(halves):
                index = sl_ref[:, h * LANES : (h + 1) * LANES]
                source = jnp.broadcast_to(spread[c : c + 1, :], (ROWS, LANES))
                cols.append(jnp.where(index > 0, pick(source, (index + (LANES - 1)) & (LANES - 1)), 0.0))
            near.append(jnp.concatenate(cols, axis=1))
        return arrived, near

    def to_sent(ys):
        for c in range(3):
            yr_ref[c] = ys[c]
        for a in range(basis):
            high, low = split(yr_ref[:, a, :])
            yw_ref[:, pl.ds(a * elems, elems)] = jnp.concatenate([high, low], axis=0)
        both = mm_nt(yw_ref[...], gs_ref[...])
        return both[0:8] + both[8:16]

    def injected(arrived):
        arr_high = arrived.astype(BF16).astype(F32)
        arr_low = arrived - arr_high
        pieces = [
            jnp.where(got_mask, part[c : c + 1, :], 0.0).astype(BF16)
            for part in (arr_high, arr_low) for c in range(3)
        ]
        both = mm_nt(jnp.concatenate(pieces, axis=0), rb_ref[...])
        return (both[0 : 3 * groups] + both[3 * groups :]) * half_inv

    def prepare_weights():
        for i in range(faces + 1):
            matrix = stiff[...] if i == 0 else lift[i - 1]
            pad_ref[i * ROWS : i * ROWS + basis, 0:basis] = jnp.dot(
                mass_inv[...], matrix, precision=HIGHEST, preferred_element_type=F32
            )
        wide = []
        for first in range(0, faces + 1, 4):
            total = None
            for i in range(first, min(first + 4, faces + 1)):
                block = pad_ref[i * ROWS : (i + 1) * ROWS, :]
                if i > first:
                    block = pltpu.roll(block, ROWS * (i - first), 1)
                total = block if total is None else total + block
            wide.append(total)
        w_high, w_low = split(jnp.concatenate(wide, axis=1))
        w_ref[0:ROWS, :] = w_high
        w_ref[ROWS : 2 * ROWS, :] = w_low
        for c in range(3):
            fg_ref[0:faces, c * ROWS : c * ROWS + basis] = face_geo[:, c, :]

    def gather_local(step):
        for v in range(fields):
            for h in range(halves):
                for f in range(faces):
                    which = jnp.broadcast_to(neighbours[f, h : h + 1, :], (ROWS, LANES))
                    low, far = which & (LANES - 1), which >> 7
                    got = None
                    for s in range(halves):
                        other = pick(u_ref[step, v * ROWS : (v + 1) * ROWS, s * LANES : (s + 1) * LANES], low)
                        got = other if got is None else jnp.where(far == s, other, got)
                    r = (v * faces + f) * ROWS
                    nb_ref[r : r + ROWS, h * LANES : (h + 1) * LANES] = got

    def gather_sent(step):
        for t in range(tiles):
            for f in range(faces):
                which = jnp.broadcast_to(nbs_ref[t, f : f + 1, :], (ROWS, LANES))
                nl_ref[t, f] = choose(step, t, which & (LANES - 1), which >> 7)

    def wait_ghosts(step):
        for k in range(4):
            ghost_copy(step, k).wait_recv()
        for t in range(tiles):
            tile = g_recv[step, 0]
            for k in range(1, 4):
                tile = jnp.where(((slot_of + (slots - t)) & 3) == k, g_recv[step, k], tile)
            gt_ref[t] = tile

    depth = (faces + 1) * ROWS

    def times(stack):
        high, low = split(jnp.concatenate(stack, axis=0))
        first = mm(w_ref[:, 0:depth], high)
        return first[0:ROWS] + (first[ROWS:] + mm(w_ref[0:ROWS, 0:depth], low))

    def advance_sent(step):
        stack = [jnp.concatenate([st_ref[step, t] for t in range(tiles)], axis=1)]
        for f in range(faces):
            cols = []
            for t in range(tiles):
                which = jnp.broadcast_to(nbs_ref[t, f : f + 1, :], (ROWS, LANES))
                at = which + jnp.where(first_of[t], ghosts * t, ghosts * (t + 4))
                got = jnp.where(which >= elems, pick(gt_ref[t], at & (LANES - 1)), nl_ref[t, f])
                cols.append(rs_ref[t, f : f + 1, :] * (got - st_ref[step, t]))
            stack.append(jnp.concatenate(cols, axis=1))
        new = times(stack)
        for t in range(tiles):
            kept = jnp.where(sent_tile[t][0:1, :] < live[0], 1.0, 0.0)
            st_ref[step + 1, t] = new[:, t * LANES : (t + 1) * LANES] * kept

    def change_of(v, step):
        u = u_ref[step, v * ROWS : (v + 1) * ROWS, :]
        stack = [u]
        for f in range(faces):
            cols = []
            r = (v * faces + f) * ROWS
            for h in range(halves):
                which = jnp.broadcast_to(neighbours[f, h : h + 1, :], (ROWS, LANES))
                got = pick(gt_ref[v // 2], (which + ghosts * (v // 2 + 4 * (v % 2))) & (LANES - 1))
                cols.append(jnp.where(which >= elems, got, nb_ref[r : r + ROWS, h * LANES : (h + 1) * LANES]))
            stack.append(rate_ref[f : f + 1, :] * (jnp.concatenate(cols, axis=1) - u))
        return times(stack)

    def finish_round(r, most):
        at = sum(len(p) for p in partners[:r])
        tile = m_send[r]
        for j in range(len(partners[r])):
            most_copy(r, j).wait_recv()
            tile = jnp.maximum(tile, m_recv[at + j])
        most = tile[0:1, 0:1]
        if r + 1 < len(partners):
            m_send[r + 1] = jnp.broadcast_to(most, (1, LANES))
            for j in range(len(partners[r + 1])):
                most_copy(r + 1, j).start()
        return most

    for sweep in range(SWEEPS - 1):
        arrived, near = gathered(sweep)
        ys = smoothed(near)
        send_sums(sweep + 1, ahead_sent + to_sent(ys))
        x_ref[...] = x_ref[...] + injected(arrived)
        sums = ahead + scatter(ys)
        x_ref[...] = 0.5 * x_ref[...] + sums * half_inv
        if sweep < SWEEPS - 2:
            ahead = scatter(smoothed(corners(lambda r: x_ref[r : r + 1, :], 3)))
            ahead_sent = at_sent(ahead)
            prepare_weights()

    geo_parts = split(fg_ref[:, 0 : 3 * ROWS])
    mv_ref[...] = x_ref[...] - x0_ref[...]
    projected = mm3(geo_parts, jnp.concatenate(corners(lambda r: mv_ref[r : r + 1, :], 3), axis=0))
    base = jnp.concatenate([rates[:, h, :] for h in range(halves)], axis=1)
    keep = jnp.where(alive, 1.0, 0.0)
    for t in range(tiles):
        low, far = sent_tile[t] & (LANES - 1), sent_tile[t] >> 7
        got = jnp.zeros((8, LANES), jnp.int32)
        for h in range(halves):
            nbp_ref[0:faces, :] = neighbours[:, h, :]
            got = jnp.where(far == h, pick(nbp_ref[...], low), got)
        nbs_ref[t] = got
    gather_sent(0)
    gather_local(0)
    wait_ghosts(0)

    arrived, near = gathered(SWEEPS - 1)
    projected = projected + mm3(geo_parts, jnp.concatenate(near, axis=0))
    rate = base * (1.0 + 0.5 * jnp.tanh(projected[0:faces])) * keep
    rate_ref[0:faces, :] = rate
    for t in range(tiles):
        low, far = sent_tile[t] & (LANES - 1), sent_tile[t] >> 7
        got = jnp.zeros((8, LANES), F32)
        for h in range(halves):
            got = jnp.where(far == h, pick(rate_ref[:, h * LANES : (h + 1) * LANES], low), got)
        rs_ref[t] = got
    advance_sent(0)
    send_ghosts(1)
    most = jnp.max(jnp.sum(rate, axis=0, keepdims=True), axis=1, keepdims=True)
    m_send[0] = jnp.broadcast_to(most, (1, LANES))
    for j in range(len(partners[0]) if rounds else 0):
        most_copy(0, j).start()
    out_c[...] = x_ref[...] + injected(arrived)

    for step in range(STEPS - 1):
        for v in range(fields):
            u_ref[step + 1, v * ROWS : (v + 1) * ROWS, :] = keep * change_of(v, step)
        if step + 2 < STEPS:
            gather_sent(step + 1)
        gather_local(step + 1)
        if step == STEPS - 2:
            for r in range(step, len(partners)):
                most = finish_round(r, most)
            scale = jnp.broadcast_to(CFL / most, (ROWS, elems))
            for v in range(fields):
                total = math.comb(STEPS, STEPS - 1) * u_ref[STEPS - 1, v * ROWS : (v + 1) * ROWS, :]
                for k in range(STEPS - 2, -1, -1):
                    total = math.comb(STEPS, k) * u_ref[k, v * ROWS : (v + 1) * ROWS, :] + scale * total
                u_ref[STEPS, v * ROWS : (v + 1) * ROWS, :] = total
        wait_ghosts(step + 1)
        if step + 2 < STEPS:
            advance_sent(step + 1)
            send_ghosts(step + 2)
        if step < min(STEPS - 2, len(partners)):
            most = finish_round(step, most)
    scale = keep * (scale * scale) * (scale * scale)
    for v in range(fields):
        new = u_ref[STEPS, v * ROWS : (v + 1) * ROWS, :] + scale * change_of(v, STEPS - 1)
        for h in range(halves):
            out_u[v * basis : (v + 1) * basis, h, :] = new[0:basis, h * LANES : (h + 1) * LANES]

    for sweep in range(SWEEPS):
        for k in range(4):
            node_copy(sweep, k).wait_send()
    for step in range(STEPS):
        for k in range(4):
            ghost_copy(step, k).wait_send()
    for r, one in enumerate(partners):
        for j in range(len(one)):
            most_copy(r, j).wait_send()


def hand_over(coords, remapped, out_c, out_u, held_c, held_u, sem):
    half = remapped.shape[0] // 2
    parts = [(coords, held_c, out_c)]
    for at in (pl.ds(0, half), pl.ds(half, remapped.shape[0] - half)):
        parts.append((remapped.at[at], held_u.at[at], out_u.at[at]))
    reads = [pltpu.make_async_copy(a, b, sem.at[0, i]) for i, (a, b, _) in enumerate(parts)]
    writes = [pltpu.make_async_copy(b, c, sem.at[1, i]) for i, (_, b, c) in enumerate(parts)]
    for one in reads:
        one.start()
    for read, write in zip(reads, writes):
        read.wait()
        write.start()
    for one in writes:
        one.wait()


def on_device(*args):
    pos, states, conn = args[:3]
    parts = lax.axis_size("dom")
    w = max(parts // 8, 1)
    shifts = (1, -1, w, -w)
    rounds = rounds_of(parts)
    total = sum(r - 1 for r, _ in rounds)
    basis, elems = conn.shape[1:]
    fields, faces = states.shape[1], args[6].shape[1]
    groups = pos.shape[2] // LANES
    nodes = pos.shape[2]
    halves = elems // LANES
    tiles = (fields + 1) // 2
    flat = list(args)
    for i, rows in ((0, 3 * groups), (1, fields * basis * halves), (2, basis * halves), (6, faces * halves), (10, faces * halves)):
        flat[i] = args[i].reshape(rows, LANES) if i == 0 else args[i].reshape(rows // halves, halves, LANES)
    for i in (3, 4, 5):
        flat[i] = args[i][0]
    vmem = pl.BlockSpec(memory_space=pltpu.VMEM)
    smem = pl.BlockSpec(memory_space=pltpu.SMEM)
    hbm = pl.BlockSpec(memory_space=pl.ANY)
    specs = [smem if i == 7 else hbm for i in range(len(args))]
    held = [pltpu.VMEM(a.shape, a.dtype) for i, a in enumerate(flat) if i != 7]
    scratch = held + [
        pltpu.SemaphoreType.DMA((len(held),)),
        pltpu.VMEM((3 * groups, LANES), F32),
        pltpu.VMEM((8 * groups, LANES), F32),
        pltpu.VMEM((ROWS, elems), jnp.int32),
        pltpu.VMEM((ROWS, elems), jnp.int32),
        pltpu.VMEM((6 * ROWS, elems), F32),
        pltpu.VMEM((6 * groups, basis * elems), BF16),
        pltpu.VMEM((LANES, basis * elems), BF16),
        pltpu.VMEM((LANES, LANES), BF16),
        pltpu.VMEM((STEPS + 1, fields * ROWS, elems), F32),
        pltpu.VMEM((fields * faces * ROWS, elems), F32),
        pltpu.VMEM((8, elems), F32),
        pltpu.VMEM(((faces + 1) * ROWS, LANES), F32),
        pltpu.VMEM((8, LANES), F32),
        pltpu.VMEM((2 * ROWS, 2 * LANES), BF16),
        pltpu.VMEM((24, LANES), jnp.int32),
        pltpu.VMEM((3 * groups, LANES), F32),
        pltpu.VMEM((8, ROWS, elems), F32),
        pltpu.VMEM((16, basis * elems), BF16),
        pltpu.VMEM((LANES, basis * elems), BF16),
        pltpu.VMEM((ROWS, elems), jnp.int32),
        pltpu.VMEM((STEPS, tiles, ROWS, LANES), F32),
        pltpu.VMEM((tiles, ROWS, LANES), F32),
        pltpu.VMEM((tiles, faces, ROWS, LANES), F32),
        pltpu.VMEM((tiles, 8, LANES), jnp.int32),
        pltpu.VMEM((tiles, 8, LANES), F32),
        pltpu.VMEM((8, LANES), jnp.int32),
        pltpu.VMEM((SWEEPS, 8, LANES), F32),
        pltpu.VMEM((SWEEPS, 4, 8, LANES), F32),
        pltpu.VMEM((STEPS, 4, ROWS, LANES), F32),
        pltpu.VMEM((STEPS, 4, ROWS, LANES), F32),
        pltpu.VMEM((max(len(rounds), 1), 1, LANES), F32),
        pltpu.VMEM((max(total, 1), 1, LANES), F32),
        pltpu.SemaphoreType.DMA((SWEEPS, 4)),
        pltpu.SemaphoreType.DMA((SWEEPS, 4)),
        pltpu.SemaphoreType.DMA((STEPS, 4)),
        pltpu.SemaphoreType.DMA((STEPS, 4)),
        pltpu.SemaphoreType.DMA((max(total, 1),)),
        pltpu.SemaphoreType.DMA((max(total, 1),)),
    ]
    coords, remapped = pl.pallas_call(
        functools.partial(kernel, parts, shifts, rounds, basis, elems, fields, faces, nodes),
        out_shape=(
            jax.ShapeDtypeStruct((3 * groups, LANES), F32),
            jax.ShapeDtypeStruct((fields * basis, halves, LANES), F32),
        ),
        in_specs=specs,
        out_specs=(vmem, vmem),
        scratch_shapes=scratch,
        compiler_params=pltpu.CompilerParams(
            collective_id=0, has_side_effects=True, vmem_limit_bytes=60 * 1024 * 1024
        ),
    )(*flat)
    coords, remapped = pl.pallas_call(
        hand_over,
        out_shape=(
            jax.ShapeDtypeStruct(coords.shape, F32),
            jax.ShapeDtypeStruct(remapped.shape, F32),
        ),
        in_specs=[hbm, hbm],
        out_specs=(hbm, hbm),
        scratch_shapes=[
            pltpu.VMEM(coords.shape, F32),
            pltpu.VMEM(remapped.shape, F32),
            pltpu.SemaphoreType.DMA((2, 3)),
        ],
        compiler_params=pltpu.CompilerParams(vmem_limit_bytes=60 * 1024 * 1024),
    )(coords, remapped)
    return coords.reshape(pos.shape), remapped.reshape(states.shape)


def solution(mesh):
    dom = lambda rank: P("dom", *([None] * (rank - 1)))
    in_specs = (
        dom(3), dom(4), dom(3), dom(3), dom(3), dom(3), dom(3), P("dom"),
        P(), P(), dom(3), P(), P(), P(),
    )
    return jax.shard_map(
        on_device, mesh=mesh, in_specs=in_specs, out_specs=(dom(3), dom(4)), check_vma=False
    )
```

time: 49 us -> 41.7 us (0.85)
  Pallas kernels: 47.5 us -> 40 us
    pallas_call x1, Pallas kernels: 45.9 us -> 38.4 us  [on_device(): pl.pallas_call(functools.partial(kernel, parts, shifts, rounds, basis, el...]
where the time goes in v2:
time: 41.7 us; the launch traced here: 41.5 us
  Pallas kernels  40 us (96%)
  between operations  1.45 us (3%)
    pallas_call x1, Pallas kernels, on_device(): pl.pallas_call(functools.partial(kernel, parts, shifts, rounds, basis, el...  38.4 us
    pallas_call x1, Pallas kernels, on_device(): pl.pallas_call(hand_over, out_shape=(jax.ShapeDtypeStruct(coords.shape, F...  1.62 us

profile of v2, /device:TPU:0, one launch (start us, length us, event | category | flops | bytes accessed | tf_op | source)
XLA Modules:
  0.0 41.5 jit_solution(16477294830723161512)
XLA Ops:
  1.3 38.4 %shard_map.149 = (f32[48,128]{1,0:T(8,128)}, f32[135,2,128]{2,1,0:T(2,128)}) custom-call(f32[48,128]{1,0:T(8,128)} %bitcast.12, f32[135,2,128]{2,1,0:T(2,128)} %bitcast.10, s32[27,2,128]{2,1,0:T(2,128)} %bitcast.11, s32[4,32]{1,0:T(4,128)} %bitcast.15, s32[4,32]{1,0:T(4,128)} %bitcast.16, s32[4,16]{1,0:T(4,128)} %bitcast.17, s32[6,2,128]{2,1,0:T(2,128)} %bitcast.13, ...), custom_call_target="tpu_custom_call" | custom-call | tf_op jit(solution)/shard_map/pallas_call | solution.py:607
  39.7 1.6 %shard_map.150 = (f32[48,128]{1,0:T(8,128)}, f32[135,2,128]{2,1,0:T(2,128)}) custom-call(f32[48,128]{1,0:T(8,128)} %get-tuple-element.6.coords, f32[135,2,128]{2,1,0:T(2,128)} %get-tuple-element.7.remapped), custom_call_target="tpu_custom_call" | custom-call | tf_op jit(solution)/shard_map/pallas_call | solution.py:620

commit v3 on v2

--- a/solution.py
+++ b/solution.py
@@ -66,10 +66,10 @@
     smooth_any, face_geo_any, rates_any, stiff_any, lift_any, mass_inv_any,
     out_c, out_u,
     x0_ref, states, conn, send_nodes, recv_nodes, send_elems, neighbours,
-    smooth, face_geo, rates, stiff, lift, mass_inv, in_sem,
+    smooth, face_geo, rates, stiff, lift, mass_inv, sent_smem, in_sem,
     x_ref, s_ref, lo_ref, hi_ref, y_ref, z_ref, b_ref, rb_ref,
     u_ref, nb_ref, rate_ref, pad_ref, fg_ref, w_ref, idx_ref,
-    mv_ref, yr_ref, yw_ref, gs_ref, sl_ref, st_ref, gt_ref, nl_ref, nbs_ref, rs_ref, nbp_ref,
+    mv_ref, cm_ref, ka_ref, kb_ref, oh_ref, hs_ref, gr_ref, tt_ref, sl_ref, st_ref, gt_ref, nl_ref, nbs_ref, rs_ref, nbp_ref,
     v_send, v_recv, g_send, g_recv, m_send, m_recv,
     vs_sem, vr_sem, gs_sem, gr_sem, ms_sem, mr_sem,
 ):
@@ -82,11 +82,11 @@
 
     sources = (
         conn_any, pos_any, states_any, send_elems_any, send_nodes_any, recv_nodes_any, smooth_any,
-        neighbours_any, rates_any, face_geo_any, mass_inv_any, stiff_any, lift_any,
+        neighbours_any, rates_any, face_geo_any, mass_inv_any, stiff_any, lift_any, send_nodes_any,
     )
     places = (
         conn, x0_ref, states, send_elems, send_nodes, recv_nodes, smooth,
-        neighbours, rates, face_geo, mass_inv, stiff, lift,
+        neighbours, rates, face_geo, mass_inv, stiff, lift, sent_smem,
     )
     loads = [
         pltpu.make_async_copy(a, b, in_sem.at[i]) for i, (a, b) in enumerate(zip(sources, places))
@@ -139,7 +139,9 @@
     hi_ref[...] = jnp.zeros(hi_ref.shape, jnp.int32)
     s_ref[...] = jnp.zeros(s_ref.shape, F32)
     u_ref[0] = jnp.zeros(u_ref.shape[1:], F32)
-    yr_ref[...] = jnp.zeros(yr_ref.shape, F32)
+    cm_ref[...] = jnp.full(cm_ref.shape, -1, jnp.int32)
+    ka_ref[...] = jnp.zeros(ka_ref.shape, F32)
+    kb_ref[...] = jnp.zeros(kb_ref.shape, F32)
     pad_ref[...] = jnp.zeros(pad_ref.shape, F32)
     fg_ref[...] = jnp.zeros(fg_ref.shape, F32)
     nbp_ref[...] = jnp.zeros(nbp_ref.shape, jnp.int32)
@@ -166,6 +168,8 @@
         part = conn[:, h, :]
         lo_ref[0:basis, h * LANES : (h + 1) * LANES] = part & (LANES - 1)
         hi_ref[0:basis, h * LANES : (h + 1) * LANES] = part >> 7
+        cm_ref[0:basis, h * LANES : (h + 1) * LANES] = part
+    cm_ref[...] = jnp.where(alive, cm_ref[...], -1)
 
     sub_lo = iota((LANES, elems), 0)
     sub_hi = iota((groups, elems), 0)
@@ -190,7 +194,7 @@
             result.append(jnp.concatenate(cols, axis=1))
         return result
 
-    def scatter(ys):
+    def scatter(ys, counting=False):
         for c in range(3):
             y_high = ys[c].astype(BF16).astype(F32)
             y_ref[c * ROWS : (c + 1) * ROWS, :] = y_high
@@ -202,8 +206,12 @@
                 z_ref[i * groups : (i + 1) * groups, at] = jnp.where(
                     chosen, y_ref[i * ROWS + a : i * ROWS + a + 1, :], 0.0
                 ).astype(BF16)
-        both = mm_nt(z_ref[...], b_ref[...])
-        return both[0 : 3 * groups] + both[3 * groups :]
+            if counting:
+                z_ref[6 * groups : 7 * groups, at] = jnp.where(chosen, one_hi, 0.0).astype(BF16)
+        rows = (7 if counting else 6) * groups
+        both = mm_nt(z_ref[0:rows, :], b_ref[...])
+        result = both[0 : 3 * groups] + both[3 * groups : 6 * groups]
+        return (result, both[6 * groups :]) if counting else result
 
     s_low = jnp.broadcast_to(sent_nodes & (LANES - 1), (8, LANES))
     s_high = jnp.broadcast_to(sent_nodes >> 7, (8, LANES))
@@ -226,16 +234,11 @@
         for k in range(4):
             node_copy(sweep, k).start()
 
-    sums = scatter(smoothed(corners(lambda r: x0_ref[r : r + 1, :], 3)))
+    sums, count = scatter(smoothed(corners(lambda r: x0_ref[r : r + 1, :], 3)), True)
     first_sent = at_sent(sums)
     pl.semaphore_wait(barrier, len(greeted))
     send_sums(0, first_sent)
 
-    for v in range(fields):
-        for h in range(halves):
-            u_ref[0, v * ROWS : v * ROWS + basis, h * LANES : (h + 1) * LANES] = states[
-                v * basis : (v + 1) * basis, h, :
-            ]
     sent_elems = jnp.broadcast_to(flat(idx_ref[16:24, :], ghosts, 4), (8, LANES))
     sent_tile = [sent_elems]
     for t in range(1, tiles):
@@ -261,20 +264,9 @@
         for k in range(4):
             ghost_copy(step, k).start()
 
-    for t in range(tiles):
-        which = jnp.broadcast_to(sent_tile[t][0:1, :], (ROWS, LANES))
-        st_ref[0, t] = choose(0, t, which & (LANES - 1), which >> 7)
-    send_ghosts(0)
-
     got_lo, got_hi = got_nodes & (LANES - 1), got_nodes >> 7
     rb_ref[...] = jnp.where(iota((LANES, LANES), 0) == got_lo, one_lo, 0.0).astype(BF16)
     got_mask = iota((groups, LANES), 0) == got_hi
-    for a in range(basis):
-        at = pl.ds(a * elems, elems)
-        z_ref[0:groups, at] = jnp.where(
-            jnp.where(alive, hi_ref[a : a + 1, :], groups) == sub_hi, one_hi, 0.0
-        ).astype(BF16)
-    count = mm_nt(z_ref[0:groups, :], b_ref[...])
     count = count + mm_nt(jnp.where(got_mask, one_hi, 0.0).astype(BF16), rb_ref[...])
     half_inv = 0.5 / jnp.maximum(count, 1.0)
     hi_at_got = jnp.zeros((8, LANES), F32)
@@ -293,25 +285,60 @@
     square = (LANES, LANES)
     got_row = jnp.broadcast_to(got_nodes, square)
     got_col = jnp.transpose(got_row)
-    sent_col = jnp.transpose(jnp.broadcast_to(sent_nodes, square))
-    same = jnp.where(got_row == got_col, one_lo, 0.0).astype(BF16)
-    marked = jnp.where((got_col & (LANES - 1)) == iota(square, 1), iota(square, 0) + 1, 0)
-    col_hi = got_col >> 7
-    table = [
-        jnp.max(jnp.where(col_hi == g, marked, 0), axis=0, keepdims=True) for g in range(groups)
-    ]
-    sl_ref[...] = corners(lambda r: table[r], 1)[0]
-    sent_wide = jnp.concatenate([sent_col] * halves, axis=1)
+    got_wide = jnp.concatenate([got_col] * halves, axis=1)
     for a in range(basis):
-        node = jnp.where(alive, (hi_ref[a : a + 1, :] << 7) + lo_ref[a : a + 1, :], -1)
-        gs_ref[:, pl.ds(a * elems, elems)] = jnp.where(sent_wide == node, one_lo, 0.0).astype(BF16)
-
-    def gathered(sweep):
+        node = cm_ref[a : a + 1, :]
+        gr_ref[:, pl.ds(a * elems, elems)] = jnp.where(got_wide == node, one_lo, 0.0).astype(BF16)
+    turned = jnp.transpose(pad_ref[0:LANES, :])[0:ROWS, :]
+    for i in range(8):
+        place = ka_ref if i < 4 else kb_ref
+        placed = turned if i % 4 == 0 else pltpu.roll(turned, ROWS * (i % 4), 1)
+        place[pl.ds(i, basis, stride=8), :] = placed[0:basis, :]
+    k8_high, k8_low = split(jnp.concatenate([ka_ref[...], kb_ref[...]], axis=1))
+    for pair in range(LANES // 16):
+        both = []
+        for part in range(2):
+            for i in range(8):
+                slot = pair * 16 + part * 8 + i
+                node = sent_smem[slot // shared, slot % shared]
+                oh_ref[part, i * ROWS : (i + 1) * ROWS, :] = jnp.where(
+                    cm_ref[...] == node, one_lo, 0.0
+                ).astype(BF16)
+            both.append(mm(k8_high, oh_ref[part]) + mm(k8_low, oh_ref[part]))
+        for b in range(basis):
+            block = jnp.concatenate([one[b * 8 : (b + 1) * 8] for one in both], axis=0)
+            high, low = split(block)
+            at = pl.ds(b * elems, elems)
+            hs_ref[pair * 16 : (pair + 1) * 16, at] = high
+            hs_ref[LANES + pair * 16 : LANES + (pair + 1) * 16, at] = low
+    response = mm_nt(hs_ref[...], gr_ref[...])
+    response = split((response[0:LANES] + response[LANES:]) * hi_at_got[0:1, :])
+    for i in range(2):
+        tt_ref[i] = response[i]
+
+    def to_sent(arrived):
+        high, low = split(arrived)
+        return mm_nt(high, tt_ref[0]) + (mm_nt(low, tt_ref[0]) + mm_nt(high, tt_ref[1]))
+
+    def prepare_slots():
+        marked = jnp.where((got_col & (LANES - 1)) == iota(square, 1), iota(square, 0) + 1, 0)
+        col_hi = got_col >> 7
+        table = [
+            jnp.max(jnp.where(col_hi == g, marked, 0), axis=0, keepdims=True) for g in range(groups)
+        ]
+        sl_ref[...] = corners(lambda r: table[r], 1)[0]
+
+    def received(sweep):
         for k in range(4):
             node_copy(sweep, k).wait_recv()
         arrived = v_recv[sweep, 0]
         for k in range(1, 4):
             arrived = jnp.where(lane // shared == k, v_recv[sweep, k], arrived)
+        return arrived
+
+    same = jnp.where(got_row == got_col, one_lo, 0.0).astype(BF16)
+
+    def gathered(arrived):
         high, low = split(arrived)
         spread = (mm(high, same) + mm(low, same)) * hi_at_got
         near = []
@@ -322,16 +349,7 @@
                 source = jnp.broadcast_to(spread[c : c + 1, :], (ROWS, LANES))
                 cols.append(jnp.where(index > 0, pick(source, (index + (LANES - 1)) & (LANES - 1)), 0.0))
             near.append(jnp.concatenate(cols, axis=1))
-        return arrived, near
-
-    def to_sent(ys):
-        for c in range(3):
-            yr_ref[c] = ys[c]
-        for a in range(basis):
-            high, low = split(yr_ref[:, a, :])
-            yw_ref[:, pl.ds(a * elems, elems)] = jnp.concatenate([high, low], axis=0)
-        both = mm_nt(yw_ref[...], gs_ref[...])
-        return both[0:8] + both[8:16]
+        return near
 
     def injected(arrived):
         arr_high = arrived.astype(BF16).astype(F32)
@@ -441,17 +459,28 @@
         return most
 
     for sweep in range(SWEEPS - 1):
-        arrived, near = gathered(sweep)
-        ys = smoothed(near)
-        send_sums(sweep + 1, ahead_sent + to_sent(ys))
+        arrived = received(sweep)
+        send_sums(sweep + 1, ahead_sent + to_sent(arrived))
+        if sweep == 0:
+            for v in range(fields):
+                for h in range(halves):
+                    u_ref[0, v * ROWS : v * ROWS + basis, h * LANES : (h + 1) * LANES] = states[
+                        v * basis : (v + 1) * basis, h, :
+                    ]
+            for t in range(tiles):
+                which = jnp.broadcast_to(sent_tile[t][0:1, :], (ROWS, LANES))
+                st_ref[0, t] = choose(0, t, which & (LANES - 1), which >> 7)
+            send_ghosts(0)
+            prepare_slots()
+        ys = smoothed(gathered(arrived))
         x_ref[...] = x_ref[...] + injected(arrived)
         sums = ahead + scatter(ys)
         x_ref[...] = 0.5 * x_ref[...] + sums * half_inv
         if sweep < SWEEPS - 2:
             ahead = scatter(smoothed(corners(lambda r: x_ref[r : r + 1, :], 3)))
             ahead_sent = at_sent(ahead)
-            prepare_weights()
-
+
+    prepare_weights()
     geo_parts = split(fg_ref[:, 0 : 3 * ROWS])
     mv_ref[...] = x_ref[...] - x0_ref[...]
     projected = mm3(geo_parts, jnp.concatenate(corners(lambda r: mv_ref[r : r + 1, :], 3), axis=0))
@@ -468,7 +497,8 @@
     gather_local(0)
     wait_ghosts(0)
 
-    arrived, near = gathered(SWEEPS - 1)
+    arrived = received(SWEEPS - 1)
+    near = gathered(arrived)
     projected = projected + mm3(geo_parts, jnp.concatenate(near, axis=0))
     rate = base * (1.0 + 0.5 * jnp.tanh(projected[0:faces])) * keep
     rate_ref[0:faces, :] = rate
@@ -563,6 +593,7 @@
     hbm = pl.BlockSpec(memory_space=pl.ANY)
     specs = [smem if i == 7 else hbm for i in range(len(args))]
     held = [pltpu.VMEM(a.shape, a.dtype) for i, a in enumerate(flat) if i != 7]
+    held.append(pltpu.SMEM(flat[3].shape, flat[3].dtype))
     scratch = held + [
         pltpu.SemaphoreType.DMA((len(held),)),
         pltpu.VMEM((3 * groups, LANES), F32),
@@ -570,7 +601,7 @@
         pltpu.VMEM((ROWS, elems), jnp.int32),
         pltpu.VMEM((ROWS, elems), jnp.int32),
         pltpu.VMEM((6 * ROWS, elems), F32),
-        pltpu.VMEM((6 * groups, basis * elems), BF16),
+        pltpu.VMEM((7 * groups, basis * elems), BF16),
         pltpu.VMEM((LANES, basis * elems), BF16),
         pltpu.VMEM((LANES, LANES), BF16),
         pltpu.VMEM((STEPS + 1, fields * ROWS, elems), F32),
@@ -581,9 +612,13 @@
         pltpu.VMEM((2 * ROWS, 2 * LANES), BF16),
         pltpu.VMEM((24, LANES), jnp.int32),
         pltpu.VMEM((3 * groups, LANES), F32),
-        pltpu.VMEM((8, ROWS, elems), F32),
-        pltpu.VMEM((16, basis * elems), BF16),
+        pltpu.VMEM((ROWS, elems), jnp.int32),
+        pltpu.VMEM((basis * 8, LANES), F32),
+        pltpu.VMEM((basis * 8, LANES), F32),
+        pltpu.VMEM((2, 8 * ROWS, elems), BF16),
+        pltpu.VMEM((2 * LANES, basis * elems), BF16),
         pltpu.VMEM((LANES, basis * elems), BF16),
+        pltpu.VMEM((2, LANES, LANES), BF16),
         pltpu.VMEM((ROWS, elems), jnp.int32),
         pltpu.VMEM((STEPS, tiles, ROWS, LANES), F32),
         pltpu.VMEM((tiles, ROWS, LANES), F32),
@@ -614,24 +649,9 @@
         out_specs=(vmem, vmem),
         scratch_shapes=scratch,
         compiler_params=pltpu.CompilerParams(
-            collective_id=0, has_side_effects=True, vmem_limit_bytes=60 * 1024 * 1024
+            collective_id=0, has_side_effects=True, vmem_limit_bytes=32 * 1024 * 1024
         ),
-    )(*flat)
-    coords, remapped = pl.pallas_call(
-        hand_over,
-        out_shape=(
-            jax.ShapeDtypeStruct(coords.shape, F32),
-            jax.ShapeDtypeStruct(remapped.shape, F32),
-        ),
-        in_specs=[hbm, hbm],
-        out_specs=(hbm, hbm),
-        scratch_shapes=[
-            pltpu.VMEM(coords.shape, F32),
-            pltpu.VMEM(remapped.shape, F32),
-            pltpu.SemaphoreType.DMA((2, 3)),
-        ],
-        compiler_params=pltpu.CompilerParams(vmem_limit_bytes=60 * 1024 * 1024),
-    )(coords, remapped)
+    )(*[a if i == 7 else pltpu.with_memory_space_constraint(a, pltpu.HBM) for i, a in enumerate(flat)])
     return coords.reshape(pos.shape), remapped.reshape(states.shape)
 
 

time: 41.7 us -> 39.7 us (0.952)
  Pallas kernels: 40 us -> 36.9 us
  local copies, waits for them, and re-layouts: 0 us -> 1.27 us
    pallas_call x1 -> x0, Pallas kernels: 1.62 us -> none  [on_device(): pl.pallas_call(hand_over, out_shape=(jax.ShapeDtypeStruct(coords.shape, F...]
    pallas_call x1, Pallas kernels: 38.4 us -> 36.9 us  [on_device(): pl.pallas_call(functools.partial(kernel, parts, shifts, rounds, basis, el...]
    unnamed x0 -> x2, local copies, waits for them, and re-layouts: none -> 1.27 us
where the time goes in v3:
time: 39.7 us; the launch traced here: 39.5 us
  Pallas kernels  36.9 us (93%)
  between operations  1.29 us (3%)
  local copies, waits for them, and re-layouts  1.27 us (3%)
    pallas_call x1, Pallas kernels, on_device(): pl.pallas_call(functools.partial(kernel, parts, shifts, rounds, basis, el...  36.9 us
    unnamed x2, local copies, waits for them, and re-layouts  1.27 us

profile of v3, /device:TPU:0, one launch (start us, length us, event | category | flops | bytes accessed | tf_op | source)
XLA Modules:
  0.0 39.5 jit_solution(15044703531504900723)
XLA Ops:
  1.3 36.9 %shard_map.149 = (f32[48,128]{1,0:T(8,128)S(1)}, f32[135,2,128]{2,1,0:T(2,128)S(1)}) custom-call(f32[48,128]{1,0:T(8,128)} %bitcast.14, f32[135,2,128]{2,1,0:T(2,128)} %bitcast.12, s32[27,2,128]{2,1,0:T(2,128)} %bitcast.13, s32[4,32]{1,0:T(4,128)} %bitcast.17, s32[4,32]{1,0:T(4,128)} %bitcast.18, s32[4,16]{1,0:T(4,128)} %bitcast.19, s32[6,2,128]{2,1,0:T(2,128)} %bitcast.15, ...), custom_call_target="tpu_custom_call" | custom-call | tf_op jit(solution)/shard_map/pallas_call | solution.py:642
  38.2 0.6 %copy.23 = f32[1,3,2048]{2,0,1:T(1,128)} copy(f32[1,3,2048]{2,0,1:T(1,128)S(1)} %bitcast.11) | data formatting | bytes 49152
  38.8 0.7 %copy.24 = f32[1,5,27,256]{3,0,2,1:T(1,128)} copy(f32[1,5,27,256]{3,0,2,1:T(1,128)S(1)} %bitcast.10) | data formatting | bytes 276480

commit v4 on v3

--- a/solution.py
+++ b/solution.py
@@ -69,7 +69,7 @@
     smooth, face_geo, rates, stiff, lift, mass_inv, sent_smem, in_sem,
     x_ref, s_ref, lo_ref, hi_ref, y_ref, z_ref, b_ref, rb_ref,
     u_ref, nb_ref, rate_ref, pad_ref, fg_ref, w_ref, idx_ref,
-    mv_ref, cm_ref, ka_ref, kb_ref, oh_ref, hs_ref, gr_ref, tt_ref, sl_ref, st_ref, gt_ref, nl_ref, nbs_ref, rs_ref, nbp_ref,
+    mv_ref, cm_ref, ka_ref, kb_ref, oh_ref, hs_ref, gr_ref, tt_ref, sl_ref, st_ref, gt_ref, nl_ref, nbs_ref, rs_ref, nbp_ref, ds_ref,
     v_send, v_recv, g_send, g_recv, m_send, m_recv,
     vs_sem, vr_sem, gs_sem, gr_sem, ms_sem, mr_sem,
 ):
@@ -81,11 +81,11 @@
     slots = LANES // ghosts
 
     sources = (
-        conn_any, pos_any, states_any, send_elems_any, send_nodes_any, recv_nodes_any, smooth_any,
+        conn_any, pos_any, send_nodes_any, recv_nodes_any, smooth_any, send_elems_any, states_any,
         neighbours_any, rates_any, face_geo_any, mass_inv_any, stiff_any, lift_any, send_nodes_any,
     )
     places = (
-        conn, x0_ref, states, send_elems, send_nodes, recv_nodes, smooth,
+        conn, x0_ref, send_nodes, recv_nodes, smooth, send_elems, states,
         neighbours, rates, face_geo, mass_inv, stiff, lift, sent_smem,
     )
     loads = [
@@ -147,7 +147,7 @@
     nbp_ref[...] = jnp.zeros(nbp_ref.shape, jnp.int32)
     rate_ref[...] = jnp.zeros(rate_ref.shape, F32)
     alive = iota((1, elems), 1) < live[0]
-    for one in loads:
+    for one in loads[:6]:
         one.wait()
 
     pad_ref[0:basis, 0:basis] = smooth[...]
@@ -239,6 +239,8 @@
     pl.semaphore_wait(barrier, len(greeted))
     send_sums(0, first_sent)
 
+    for one in loads[6:]:
+        one.wait()
     sent_elems = jnp.broadcast_to(flat(idx_ref[16:24, :], ghosts, 4), (8, LANES))
     sent_tile = [sent_elems]
     for t in range(1, tiles):
@@ -278,9 +280,6 @@
         )
     half_inv = jnp.concatenate([half_inv] * 3, axis=0)
 
-    x_ref[...] = 0.5 * x0_ref[...] + sums * half_inv
-    ahead = scatter(smoothed(corners(lambda r: x_ref[r : r + 1, :], 3)))
-    ahead_sent = at_sent(ahead)
 
     square = (LANES, LANES)
     got_row = jnp.broadcast_to(got_nodes, square)
@@ -316,6 +315,10 @@
     for i in range(2):
         tt_ref[i] = response[i]
 
+    x_ref[...] = 0.5 * x0_ref[...] + sums * half_inv
+    ahead = scatter(smoothed(corners(lambda r: x_ref[r : r + 1, :], 3)))
+    ahead_sent = at_sent(ahead)
+
     def to_sent(arrived):
         high, low = split(arrived)
         return mm_nt(high, tt_ref[0]) + (mm_nt(low, tt_ref[0]) + mm_nt(high, tt_ref[1]))
@@ -417,20 +420,45 @@
         first = mm(w_ref[:, 0:depth], high)
         return first[0:ROWS] + (first[ROWS:] + mm(w_ref[0:ROWS, 0:depth], low))
 
+    def prepare_sent():
+        for f in range(faces):
+            cols = []
+            for t in range(tiles):
+                cols.append(neighbour_of_sent(0, t, f) - st_ref[0, t])
+            ds_ref[f + 1] = one_face(f + 1, jnp.concatenate(cols, axis=1))
+        ds_ref[0] = one_face(0, jnp.concatenate([st_ref[0, t] for t in range(tiles)], axis=1))
+
+    def one_face(i, value):
+        at = i * ROWS
+        return mm3((w_ref[0:ROWS, at : at + ROWS], w_ref[ROWS : 2 * ROWS, at : at + ROWS]), value)
+
+    def kept_sent(t):
+        return jnp.where(sent_tile[t][0:1, :] < live[0], 1.0, 0.0)
+
+    def first_sent_step():
+        for t in range(tiles):
+            at = pl.ds(t * LANES, LANES)
+            new = ds_ref[0, :, at]
+            for f in range(faces):
+                new = new + rs_ref[t, f : f + 1, :] * ds_ref[f + 1, :, at]
+            st_ref[1, t] = new * kept_sent(t)
+
+    def neighbour_of_sent(step, t, f):
+        which = jnp.broadcast_to(nbs_ref[t, f : f + 1, :], (ROWS, LANES))
+        at = which + jnp.where(first_of[t], ghosts * t, ghosts * (t + 4))
+        return jnp.where(which >= elems, pick(gt_ref[t], at & (LANES - 1)), nl_ref[t, f])
+
     def advance_sent(step):
         stack = [jnp.concatenate([st_ref[step, t] for t in range(tiles)], axis=1)]
         for f in range(faces):
             cols = []
             for t in range(tiles):
-                which = jnp.broadcast_to(nbs_ref[t, f : f + 1, :], (ROWS, LANES))
-                at = which + jnp.where(first_of[t], ghosts * t, ghosts * (t + 4))
-                got = jnp.where(which >= elems, pick(gt_ref[t], at & (LANES - 1)), nl_ref[t, f])
+                got = neighbour_of_sent(step, t, f)
                 cols.append(rs_ref[t, f : f + 1, :] * (got - st_ref[step, t]))
             stack.append(jnp.concatenate(cols, axis=1))
         new = times(stack)
         for t in range(tiles):
-            kept = jnp.where(sent_tile[t][0:1, :] < live[0], 1.0, 0.0)
-            st_ref[step + 1, t] = new[:, t * LANES : (t + 1) * LANES] * kept
+            st_ref[step + 1, t] = new[:, t * LANES : (t + 1) * LANES] * kept_sent(t)
 
     def change_of(v, step):
         u = u_ref[step, v * ROWS : (v + 1) * ROWS, :]
@@ -496,6 +524,7 @@
     gather_sent(0)
     gather_local(0)
     wait_ghosts(0)
+    prepare_sent()
 
     arrived = received(SWEEPS - 1)
     near = gathered(arrived)
@@ -508,7 +537,7 @@
         for h in range(halves):
             got = jnp.where(far == h, pick(rate_ref[:, h * LANES : (h + 1) * LANES], low), got)
         rs_ref[t] = got
-    advance_sent(0)
+    first_sent_step()
     send_ghosts(1)
     most = jnp.max(jnp.sum(rate, axis=0, keepdims=True), axis=1, keepdims=True)
     m_send[0] = jnp.broadcast_to(most, (1, LANES))
@@ -554,19 +583,14 @@
             most_copy(r, j).wait_send()
 
 
-def hand_over(coords, remapped, out_c, out_u, held_c, held_u, sem):
-    half = remapped.shape[0] // 2
-    parts = [(coords, held_c, out_c)]
-    for at in (pl.ds(0, half), pl.ds(half, remapped.shape[0] - half)):
-        parts.append((remapped.at[at], held_u.at[at], out_u.at[at]))
-    reads = [pltpu.make_async_copy(a, b, sem.at[0, i]) for i, (a, b, _) in enumerate(parts)]
-    writes = [pltpu.make_async_copy(b, c, sem.at[1, i]) for i, (_, b, c) in enumerate(parts)]
-    for one in reads:
+def hand_over(coords, remapped, out_c, out_u, sem):
+    moves = [
+        pltpu.make_async_copy(remapped, out_u, sem.at[0]),
+        pltpu.make_async_copy(coords, out_c, sem.at[1]),
+    ]
+    for one in moves:
         one.start()
-    for read, write in zip(reads, writes):
-        read.wait()
-        write.start()
-    for one in writes:
+    for one in moves:
         one.wait()
 
 
@@ -626,6 +650,7 @@
         pltpu.VMEM((tiles, 8, LANES), jnp.int32),
         pltpu.VMEM((tiles, 8, LANES), F32),
         pltpu.VMEM((8, LANES), jnp.int32),
+        pltpu.VMEM((faces + 1, ROWS, tiles * LANES), F32),
         pltpu.VMEM((SWEEPS, 8, LANES), F32),
         pltpu.VMEM((SWEEPS, 4, 8, LANES), F32),
         pltpu.VMEM((STEPS, 4, ROWS, LANES), F32),
@@ -652,6 +677,14 @@
             collective_id=0, has_side_effects=True, vmem_limit_bytes=32 * 1024 * 1024
         ),
     )(*[a if i == 7 else pltpu.with_memory_space_constraint(a, pltpu.HBM) for i, a in enumerate(flat)])
+    coords, remapped = pl.pallas_call(
+        hand_over,
+        out_shape=(pltpu.HBM(coords.shape, F32), pltpu.HBM(remapped.shape, F32)),
+        in_specs=[vmem, vmem],
+        out_specs=(hbm, hbm),
+        scratch_shapes=[pltpu.SemaphoreType.DMA((2,))],
+        compiler_params=pltpu.CompilerParams(vmem_limit_bytes=1024 * 1024),
+    )(coords, remapped)
     return coords.reshape(pos.shape), remapped.reshape(states.shape)
 
 

time: 39.7 us -> 37.3 us (0.940)
  local copies, waits for them, and re-layouts: 1.27 us -> 0 us
  Pallas kernels: 36.9 us -> 35.7 us
    pallas_call x1, Pallas kernels: 36.9 us -> 35.1 us  [on_device(): pl.pallas_call(functools.partial(kernel, parts, shifts, rounds, basis, el...]
    unnamed x2 -> x0, local copies, waits for them, and re-layouts: 1.27 us -> none
    pallas_call x0 -> x1, Pallas kernels: none -> 0.68 us  [on_device(): pl.pallas_call(hand_over, out_shape=(pltpu.HBM(coords.shape, F32), pltpu....]
where the time goes in v4:
time: 37.3 us; the launch traced here: 37.2 us
  Pallas kernels  35.7 us (96%)
  between operations  1.45 us (4%)
    pallas_call x1, Pallas kernels, on_device(): pl.pallas_call(functools.partial(kernel, parts, shifts, rounds, basis, el...  35.1 us

profile of v4, /device:TPU:0, one launch (start us, length us, event | category | flops | bytes accessed | tf_op | source)
XLA Modules:
  0.0 37.2 jit_solution(5324949212586660119)
XLA Ops:
  1.3 35.1 %shard_map.149 = (f32[48,128]{1,0:T(8,128)S(1)}, f32[135,2,128]{2,1,0:T(2,128)S(1)}) custom-call(f32[48,128]{1,0:T(8,128)} %bitcast.12, f32[135,2,128]{2,1,0:T(2,128)} %bitcast.10, s32[27,2,128]{2,1,0:T(2,128)} %bitcast.11, s32[4,32]{1,0:T(4,128)} %bitcast.15, s32[4,32]{1,0:T(4,128)} %bitcast.16, s32[4,16]{1,0:T(4,128)} %bitcast.17, s32[6,2,128]{2,1,0:T(2,128)} %bitcast.13, ...), custom_call_target="tpu_custom_call" | custom-call | tf_op jit(solution)/shard_map/pallas_call | solution.py:667
  36.4 0.7 %shard_map.150 = (f32[48,128]{1,0:T(8,128)}, f32[135,2,128]{2,1,0:T(2,128)}) custom-call(f32[48,128]{1,0:T(8,128)S(1)} %get-tuple-element.6.coords, f32[135,2,128]{2,1,0:T(2,128)S(1)} %get-tuple-element.7.remapped), custom_call_target="tpu_custom_call" | custom-call | tf_op jit(solution)/shard_map/pallas_call | solution.py:680

commit v5 on v4

--- a/solution.py
+++ b/solution.py
@@ -174,9 +174,6 @@
     sub_lo = iota((LANES, elems), 0)
     sub_hi = iota((groups, elems), 0)
     one_lo, one_hi = jnp.float32(1.0), jnp.float32(1.0)
-    for a in range(basis):
-        at = pl.ds(a * elems, elems)
-        b_ref[:, at] = jnp.where(sub_lo == lo_ref[a : a + 1, :], one_lo, 0.0).astype(BF16)
 
     def corners(row_of, count):
         result = []
@@ -234,7 +231,13 @@
         for k in range(4):
             node_copy(sweep, k).start()
 
-    sums, count = scatter(smoothed(corners(lambda r: x0_ref[r : r + 1, :], 3)), True)
+    near = []
+    for c in range(3):
+        near += corners(lambda r: x0_ref[c * groups + r : c * groups + r + 1, :], 1)
+        for a in range(c * basis // 3, (c + 1) * basis // 3):
+            at = pl.ds(a * elems, elems)
+            b_ref[:, at] = jnp.where(sub_lo == lo_ref[a : a + 1, :], one_lo, 0.0).astype(BF16)
+    sums, count = scatter(smoothed(near), True)
     first_sent = at_sent(sums)
     pl.semaphore_wait(barrier, len(greeted))
     send_sums(0, first_sent)

time: 37.3 us -> 37.4 us (level)
  no operation moved by 1% of the time
where the time goes in v5:
time: 37.4 us; the launch traced here: 37.2 us
  Pallas kernels  35.8 us (96%)
  between operations  1.45 us (4%)
    pallas_call x1, Pallas kernels, on_device(): pl.pallas_call(functools.partial(kernel, parts, shifts, rounds, basis, el...  35.1 us

profile of v5, /device:TPU:0, one launch (start us, length us, event | category | flops | bytes accessed | tf_op | source)
XLA Modules:
  0.0 37.2 jit_solution(18203961201490588779)
XLA Ops:
  1.3 35.1 %shard_map.149 = (f32[48,128]{1,0:T(8,128)S(1)}, f32[135,2,128]{2,1,0:T(2,128)S(1)}) custom-call(f32[48,128]{1,0:T(8,128)} %bitcast.12, f32[135,2,128]{2,1,0:T(2,128)} %bitcast.10, s32[27,2,128]{2,1,0:T(2,128)} %bitcast.11, s32[4,32]{1,0:T(4,128)} %bitcast.15, s32[4,32]{1,0:T(4,128)} %bitcast.16, s32[4,16]{1,0:T(4,128)} %bitcast.17, s32[6,2,128]{2,1,0:T(2,128)} %bitcast.13, ...), custom_call_target="tpu_custom_call" | custom-call | tf_op jit(solution)/shard_map/pallas_call | solution.py:670
  36.4 0.7 %shard_map.150 = (f32[48,128]{1,0:T(8,128)}, f32[135,2,128]{2,1,0:T(2,128)}) custom-call(f32[48,128]{1,0:T(8,128)S(1)} %get-tuple-element.6.coords, f32[135,2,128]{2,1,0:T(2,128)S(1)} %get-tuple-element.7.remapped), custom_call_target="tpu_custom_call" | custom-call | tf_op jit(solution)/shard_map/pallas_call | solution.py:683
